TPU v7x, 512 devices: a whole 4x8x8 slice. The times are simulated.
512 devices in a mesh: dp: 64 (over x, y, core), mp: 8 (over z).
Axes of the slice: x: 4, y: 8, z: 8, core: 2. Of those that a mesh axis runs over, the one named last changes fastest.
Arguments:
- tokens: bfloat16 [49152, 6144], P('dp', 'mp'), may hold values from -12 to 12, as said below
- cotangent: bfloat16 [49152, 512], P('dp'), may hold values from -12 to 12, as said below
- weights: float32 [6144, 512], P(('mp', 'dp')), may hold values from -0.078125 to 0.078125
- moment_one: float32 [6144, 512], P(('mp', 'dp')), may hold values from -3 to 3
- moment_two: float32 [6144, 512], P(('mp', 'dp')), may hold values from 0.05 to 2
Outputs:
- new_weights: float32 [6144, 512], P(('mp', 'dp'))
- new_moment_one: float32 [6144, 512], P(('mp', 'dp'))
- new_moment_two: float32 [6144, 512], P(('mp', 'dp'))
Inputs may be any that keep to these rules, and one draw needn't show every extreme that they name: `tokens`: Real-valued activations. `cotangent`: Real-valued cotangents.
All inputs are finite; a program needn't handle non-finite values.
Results may differ from a plain program's by a relative error of at most 0.0045.
Values may be sent and summed in bfloat16 or wider, within the bound.
No kernel may reach another device: no remote copies, remote signals or barrier semaphores. Data moves between devices by JAX's collectives and lax.ppermute only.
A program may use at most 64 MiB of HBM per device.

v0:
```python
import math

import jax
import jax.numpy as jnp
from jax import lax
from jax.sharding import PartitionSpec as P

HEAD_DIM = 128


radius = 8.0
rate = 0.005
decay_one = 0.9
decay_two = 0.95
weight_decay = 0.1
step_count = 10


def head_norm(values):
    shaped = values.reshape(values.shape[0], -1, HEAD_DIM)
    centred = shaped - jnp.mean(shaped, axis=-1, keepdims=True)
    spread = jnp.mean(centred * centred, axis=-1, keepdims=True)
    return (centred * lax.rsqrt(spread + 1e-06)).reshape(values.shape)


def finish_heads(partial_value, cotangent):
    queries = lax.psum(partial_value.astype(jnp.bfloat16), "mp").astype(jnp.float32)
    _, backward = jax.vjp(head_norm, queries)
    (result,) = backward(cotangent.astype(jnp.float32))
    return result.astype(jnp.bfloat16)


def weight_terms(tokens, grads, loss_scale):
    summed = lax.dot_general(
        tokens, grads, (((0,), (0,)), ((), ())), preferred_element_type=jnp.float32
    )
    return summed * loss_scale


def local(tokens, cotangent, weights, moment_one, moment_two):
    loss_scale = 1.0 / math.sqrt(tokens.shape[0] * lax.axis_size("dp"))

    def add_piece(piece):
        return jnp.dot(tokens, piece, preferred_element_type=jnp.float32)

    partial_value = add_piece(
        lax.all_gather(weights.astype(jnp.bfloat16), "dp", axis=0, tiled=True)
    )
    first_heads = finish_heads(partial_value, cotangent)
    first = lax.psum_scatter(
        weight_terms(tokens, first_heads, loss_scale), "dp", scatter_dimension=0, tiled=True
    )
    squares = lax.psum(jnp.sum(first * first), ("dp", "mp"))
    perturbed = weights + radius * first / jnp.sqrt(squares + 1e-06)
    partial_two = add_piece(
        lax.all_gather(perturbed.astype(jnp.bfloat16), "dp", axis=0, tiled=True)
    )
    second_heads = finish_heads(partial_two, cotangent)
    second = lax.psum_scatter(
        weight_terms(tokens, second_heads, loss_scale), "dp", scatter_dimension=0, tiled=True
    )
    new_moment_one = decay_one * moment_one + (1.0 - decay_one) * second
    new_moment_two = decay_two * moment_two + (1.0 - decay_two) * second * second
    correct_one = 1.0 - decay_one**step_count
    correct_two = 1.0 - decay_two**step_count
    update = new_moment_one / correct_one / (jnp.sqrt(new_moment_two / correct_two) + 1e-08)
    new_weights = weights - rate * (update + weight_decay * weights)
    return (new_weights, new_moment_one, new_moment_two)


def solution(mesh):
    in_specs = (
        P("dp", "mp"),
        P("dp", None),
        P(("mp", "dp"), None),
        P(("mp", "dp"), None),
        P(("mp", "dp"), None),
    )
    out_specs = (P(("mp", "dp"), None), P(("mp", "dp"), None), P(("mp", "dp"), None))
    return jax.shard_map(local, mesh=mesh, in_specs=in_specs, out_specs=out_specs, check_vma=False)
```

profile of v0, /device:TPU:1, one launch (start us, length us, event | category | flops | bytes accessed | tf_op | source)
XLA Modules:
  0.0 851.6 jit_solution(2472543443999596622)
XLA Ops:
  8.1 53.8 %all-gather = bf16[64,12,512]{2,1,0:T(8,128)(2,1)S(1)} all-gather(bf16[1,12,512]{2,1,0:T(8,128)(2,1)S(1)} %convert_bitcast_fusion), channel_id=1, replica_groups=mesh['dp'=64,'mp'=8] {'dp'}, dimensions={0}, use_global_device_ids=true | all-gather | bytes 798720 | tf_op jit(solution)/shard_map/all_gather | solution.py:47
  64.4 75.8 %all-reduce.7.cloned.1.call-done = bf16[768,512]{1,0:T(8,128)(2,1)} async-done(((bf16[768,512]{1,0:T(8,128)(2,1)}), bf16[768,512]{1,0:T(8,128)(2,1)}) %all-reduce.7.cloned.1.call-update) | async-done | bytes 786448 | tf_op jit(solution)/shard_map/psum | solution.py:27
  140.2 2.6 reshape.74
  142.8 3.1 reduce_sum.78
  146.9 6.1 multiply_reduce_fusion.3
  154.1 1.8 copy.63
  158.8 1.6 copy.64
  160.5 5.9 fusion.2
  170.3 2.6 multiply_bitcast_fusion.1
  175.0 197.9 %all-reduce.11.cloned.1.call-done = f32[768,512]{0,1:T(8,128)} async-done(((f32[768,512]{0,1:T(8,128)}), f32[768,512]{0,1:T(8,128)}) %all-reduce.11.cloned.1.call-update) | async-done | bytes 1572880
  372.9 2.5 multiply_reduce_fusion.4
  375.4 1.7 copy.67
  377.0 100.1 %psum.22 = f32[]{:T(128)} all-reduce(f32[]{:T(128)} %get-tuple-element.19), channel_id=1, replica_groups=mesh['dp'=64,'mp'=8] {'dp','mp'}, use_global_device_ids=true, to_apply=%region_7.0 | all-reduce | flops 1 | bytes 8 | tf_op jit(solution)/shard_map/psum | solution.py:53
  478.6 54.5 %all-gather.1 = bf16[64,12,512]{2,1,0:T(8,128)(2,1)} all-gather(bf16[1,12,512]{2,1,0:T(8,128)(2,1)S(1)} %fusion.14), channel_id=1, replica_groups=mesh['dp'=64,'mp'=8] {'dp'}, dimensions={0}, use_global_device_ids=true | all-gather | bytes 798720 | tf_op jit(solution)/shard_map/all_gather | solution.py:56
  533.1 2.1 reshape.80
  535.2 2.8 fusion.6
  538.0 72.3 %all-reduce.9.cloned.1.call-done = bf16[768,512]{1,0:T(8,128)(2,1)} async-done(((bf16[768,512]{1,0:T(8,128)(2,1)}), bf16[768,512]{1,0:T(8,128)(2,1)}) %all-reduce.9.cloned.1.call-update) | async-done | bytes 786448 | tf_op jit(solution)/shard_map/psum | solution.py:27
  610.4 2.6 reshape.76
  613.0 3.1 reduce_sum.86
  617.1 6.1 multiply_reduce_fusion.1
  624.3 1.8 copy.73
  630.7 5.9 fusion.5
  640.6 2.6 multiply_bitcast_fusion
  643.2 199.9 %all-reduce.13.cloned.1.call-done = f32[768,512]{0,1:T(8,128)} async-done(((f32[768,512]{0,1:T(8,128)}), f32[768,512]{0,1:T(8,128)}) %all-reduce.13.cloned.1.call-update) | async-done | bytes 1572880
  (66 shorter events, 27.1 us)
Async XLA Ops:
  7.2 54.9 %copy-start = (bf16[768,768]{1,0:T(8,128)(2,1)S(1)}, bf16[768,768]{1,0:T(8,128)(2,1)}, u32[]{:S(2)}) copy-start(bf16[768,768]{1,0:T(8,128)(2,1)} %param.5) | copy-start | bytes 3538948
  7.2 133.0 %all-reduce.7.cloned.1.call-start = ((), (), s32[]{:S(2)}) async-start(), calls=%async_computation | async-start | bytes 1572864 | tf_op jit(solution)/shard_map/psum | solution.py:27
  62.1 1.7 copy-start.1
  63.8 309.1 %all-reduce.11.cloned.1.call-start = ((), (), s32[]{:S(2)}) async-start(), calls=%async_computation.2 | async-start | bytes 3145728
  146.9 6.1 copy-start.4
  166.3 1.0 copy-start.7
  166.4 2.0 copy-start.9
  167.4 2.0 copy-start.5
  168.4 2.0 copy-start.11
  173.0 437.4 %all-reduce.9.cloned.1.call-start = ((), (), s32[]{:S(2)}) async-start(), calls=%async_computation.1 | async-start | bytes 1572864 | tf_op jit(solution)/shard_map/psum | solution.py:27
  538.0 305.1 %all-reduce.13.cloned.1.call-start = ((), (), s32[]{:S(2)}) async-start(), calls=%async_computation.3 | async-start | bytes 3145728
  617.1 6.1 copy-start.2
  636.5 1.0 copy-start.6
  636.6 2.0 copy-start.8
  637.6 2.0 copy-start.3
  638.6 2.0 copy-start.10
  643.2 201.2 %copy-start.12 = (f32[12,512]{1,0:T(8,128)S(1)}, f32[12,512]{1,0:T(8,128)}, u32[]{:S(2)}) copy-start(f32[12,512]{1,0:T(8,128)} %param.7) | copy-start | bytes 73732
  643.2 201.2 %copy-start.13 = (f32[12,512]{1,0:T(8,128)S(1)}, f32[12,512]{1,0:T(8,128)}, u32[]{:S(2)}) copy-start(f32[12,512]{1,0:T(8,128)} %param.8) | copy-start | bytes 73732
  643.2 201.2 %copy-start.14 = (f32[12,512]{1,0:T(8,128)S(1)}, f32[12,512]{1,0:T(8,128)}, u32[]{:S(2)}) copy-start(f32[12,512]{1,0:T(8,128)} %param.9) | copy-start | bytes 73732
Sparse Core Ops, SparseCore 0:
  63.9 76.2 all-reduce.6
  173.1 199.6 all-reduce.10
  538.1 72.2 all-reduce.8
  643.3 199.7 all-reduce.12
where the time goes:
time: 855 us; the launch traced here: 852 us
  waiting for transfers between devices  546 us (64%)
  blocking collectives  208 us (24%)
  other arithmetic  39.5 us (5%)
  local copies, waits for them, and re-layouts  32.4 us (4%)
  between operations  15.4 us (2%)
  matrix products  9.7 us (1%)
    unnamed x6, waiting for transfers between devices  398 us
    psum x2, waiting for transfers between devices, finish_heads(): lax.psum(partial_value.astype(jnp.bfloat16), 'mp').astype(jnp.float32)  148 us
    psum x1, blocking collectives, local(): squares = lax.psum(jnp.sum(first * first), ('dp', 'mp'))  100 us
    all_gather x1, blocking collectives, local(): lax.all_gather(perturbed.astype(jnp.bfloat16), 'dp', axis=0, tiled=True)  54.5 us
    all_gather x1, blocking collectives, local(): lax.all_gather(weights.astype(jnp.bfloat16), 'dp', axis=0, tiled=True)  53.8 us
    reduce_sum x4, other arithmetic, head_norm(): centred = shaped - jnp.mean(shaped, axis=-1, keepdims=True)  17.8 us
  transfers between devices with their start and end apart: 4, of which 4 were waited for; matrix products, arithmetic and copies ran while one was open for 0% of the time, Pallas kernels for 0%

commit v1 on v0

v1 whole, which is shorter than its diff:
```python
import math

import jax
import jax.numpy as jnp
from jax import lax
from jax.experimental import pallas as pl
from jax.experimental.pallas import tpu as pltpu
from jax.sharding import Mesh
from jax.sharding import PartitionSpec as P

HEAD_DIM = 128
CHUNKS = 1
PAD = 16
CORES = 2

radius = 8.0
rate = 0.005
decay_one = 0.9
decay_two = 0.95
weight_decay = 0.1
step_count = 10

BF16 = jnp.bfloat16
F32 = jnp.float32


def pieces_of(value, shape, row):
    high = value.astype(BF16).astype(F32)
    rest = value - high
    middle = rest.astype(BF16).astype(F32)
    low = rest - middle
    rows = lax.broadcasted_iota(jnp.int32, shape, len(shape) - 2)
    lanes = lax.broadcasted_iota(jnp.int32, shape, len(shape) - 1)
    picked = jnp.where(lanes == 0, high, jnp.where(lanes == 1, middle, jnp.where(lanes == 2, low, 0.0)))
    return jnp.where(rows == row, picked, 0.0)


def head_kernel(partial_ref, base_ref, scale_ref, cotangent_ref, queries_ref, out_ref):
    tokens = queries_ref.shape[0]
    width = queries_ref.shape[1]
    scale = scale_ref[0, 0]
    for head in range(width // HEAD_DIM):
        lanes = slice(head * HEAD_DIM, (head + 1) * HEAD_DIM)
        total = partial_ref[0, 0:tokens, lanes].astype(F32)
        for part in range(1, partial_ref.shape[0]):
            total = total + partial_ref[part, 0:tokens, lanes].astype(F32)
        queries = total * scale + base_ref[:, lanes]
        queries_ref[:, lanes] = queries
        cotangent = cotangent_ref[:, lanes].astype(F32)
        centred = queries - jnp.mean(queries, axis=-1, keepdims=True)
        spread = jnp.mean(centred * centred, axis=-1, keepdims=True)
        factor = lax.rsqrt(spread + 1e-06)
        normed = centred * factor
        level = jnp.mean(cotangent, axis=-1, keepdims=True)
        along = jnp.mean(cotangent * normed, axis=-1, keepdims=True)
        out_ref[:, lanes] = (factor * (cotangent - level - normed * along)).astype(BF16)


def head_step(partials, base, scale, cotangent):
    tokens, width = cotangent.shape
    vmem = pl.BlockSpec(memory_space=pltpu.VMEM)
    return pl.pallas_call(
        head_kernel,
        in_specs=[vmem, vmem, pl.BlockSpec(memory_space=pltpu.SMEM), vmem],
        out_specs=[vmem, vmem],
        out_shape=[
            jax.ShapeDtypeStruct((tokens, width), F32),
            jax.ShapeDtypeStruct((tokens, width), BF16),
        ],
        name="head_grad",
    )(partials, base, scale.reshape(1, 1), cotangent)


def local(tokens, cotangent, weights, moment_one, moment_two):
    count, depth = tokens.shape
    rows, columns = weights.shape
    groups = lax.axis_size("q")
    parts = lax.axis_size("mp")
    loss_scale = 1.0 / math.sqrt(count * groups * CORES)
    core = lax.axis_index("c")
    share = count // parts
    width = columns // CHUNKS
    half = groups * PAD

    feature = lax.broadcasted_iota(jnp.int32, (depth, CORES * half), 0)
    slot = lax.broadcasted_iota(jnp.int32, (depth, CORES * half), 1)
    owner = slot // half
    place = slot % half
    source = jnp.where(owner == 0, core, 1 - core)
    target = ((place // PAD) * CORES + source) * rows + place % PAD
    choose = ((feature == target) & (place % PAD < rows)).astype(BF16)
    spread_tokens = jnp.dot(tokens, choose, preferred_element_type=F32).astype(BF16)
    mine, other = spread_tokens[:, :half], spread_tokens[:, half:]

    cot = lax.dynamic_slice_in_dim(cotangent, lax.axis_index("mp") * share, share, 0)
    swap = [(0, 1), (1, 0)]

    def cut(array, chunk):
        return array[..., chunk * width : (chunk + 1) * width]

    def gather_rows(block):
        block = jnp.broadcast_to(block[None], (groups, PAD, width))
        own = lax.all_to_all(block, "q", 0, 0)
        return own, lax.ppermute(own, "c", swap)

    def queries_of(own, theirs):
        value = jnp.dot(mine, own.reshape(half, width), preferred_element_type=F32)
        value = value + jnp.dot(other, theirs.reshape(half, width), preferred_element_type=F32)
        return value.astype(BF16).reshape(parts, share, width)

    def gradient_of(grads):
        grads = lax.all_gather(grads, "mp", axis=0, tiled=True)

        def product(side):
            return lax.dot_general(side, grads, (((0,), (0,)), ((), ())), preferred_element_type=F32)

        theirs = lax.ppermute(product(other).astype(BF16), "c", swap)
        summed = (product(mine) + theirs.astype(F32)).astype(BF16)
        received = lax.all_to_all(summed.reshape(groups, PAD, width), "q", 0, 0)
        return jnp.sum(received.astype(F32), axis=0) * loss_scale

    one = jnp.ones((), F32)
    zeros = jnp.zeros((share, width), F32)
    padded = jnp.pad(weights.astype(BF16), ((0, PAD - rows), (0, 0)))
    gathered = [gather_rows(cut(padded, k)) for k in range(CHUNKS)]
    partials = [lax.all_to_all(queries_of(*pair), "mp", 0, 0) for pair in gathered]
    heads = [head_step(partials[k], zeros, one, cut(cot, k)) for k in range(CHUNKS)]
    queries = [pair[0] for pair in heads]
    firsts = [gradient_of(pair[1]) for pair in heads]

    exchanged = []
    squares = jnp.zeros((), F32)
    for first in firsts:
        block = first + pieces_of(jnp.sum(first * first), (PAD, width), rows)
        own, theirs = gather_rows(block.astype(BF16))
        total = jnp.sum(own[:, rows, :3].astype(F32)) + jnp.sum(theirs[:, rows, :3].astype(F32))
        tail = jnp.broadcast_to(pieces_of(total, (8, width), 0).astype(BF16), (parts, 8, width))
        sent = jnp.concatenate([queries_of(own, theirs), tail], axis=1)
        received = lax.all_to_all(sent, "mp", 0, 0)
        squares = squares + jnp.sum(received[:, share, :3].astype(F32))
        exchanged.append(received)
    scale = radius / jnp.sqrt(squares + 1e-06)
    seconds = [
        gradient_of(head_step(exchanged[k], queries[k], scale, cut(cot, k))[1]) for k in range(CHUNKS)
    ]
    second = jnp.concatenate(seconds, axis=1)[:rows]

    new_moment_one = decay_one * moment_one + (1.0 - decay_one) * second
    new_moment_two = decay_two * moment_two + (1.0 - decay_two) * second * second
    correct_one = 1.0 - decay_one**step_count
    correct_two = 1.0 - decay_two**step_count
    update = new_moment_one / correct_one / (jnp.sqrt(new_moment_two / correct_two) + 1e-08)
    new_weights = weights - rate * (update + weight_decay * weights)
    return (new_weights, new_moment_one, new_moment_two)


def solution(mesh):
    groups = mesh.shape["dp"] // CORES
    fine = Mesh(mesh.devices.reshape(groups, CORES, mesh.shape["mp"]), ("q", "c", "mp"))
    dp = ("q", "c")
    shard = P(("mp", "q", "c"), None)
    in_specs = (P(dp, "mp"), P(dp, None), shard, shard, shard)
    return jax.shard_map(local, mesh=fine, in_specs=in_specs, out_specs=(shard, shard, shard), check_vma=False)
```

time: 855 us -> 250 us (0.29)
  waiting for transfers between devices: 546 us -> 53.5 us
  blocking collectives: 208 us -> 110 us
  starting transfers between devices: 0.16 us -> 53.5 us
  other arithmetic: 39.5 us -> 4.39 us
  local copies, waits for them, and re-layouts: 32.4 us -> 5.44 us
  between operations: 15.4 us -> 4.23 us
    unnamed x6 -> x0, waiting for transfers between devices: 398 us -> none
    psum x2 -> x0, waiting for transfers between devices: 148 us -> none  [finish_heads(): lax.psum(partial_value.astype(jnp.bfloat16), 'mp').astype(jnp.float32)]
    psum x1 -> x0, blocking collectives: 100 us -> none  [local(): squares = lax.psum(jnp.sum(first * first), ('dp', 'mp'))]
    all_to_all x0 -> x3, blocking collectives: none -> 68.5 us  [the longest x1 27.4 us: local(): received = lax.all_to_all(sent, 'mp', 0, 0)]
    all_gather x2, blocking collectives: 108 us -> 41.1 us  [gradient_of(): grads = lax.all_gather(grads, 'mp', axis=0, tiled=True)]
    all_to_all x0 -> x3, waiting for transfers between devices: none -> 50.5 us  [the longest x1 22.1 us: local(): lax.all_to_all(queries_of(*pair), 'mp', 0, 0)]
    reduce_sum x7 -> x6, other arithmetic: 32.4 us -> 2.6 us  [the longest x1 0.61 us: local(): jnp.sum(own[:, rows, :3].astype(F32))]
    ppermute x0 -> x4, starting transfers between devices: none -> 27.7 us  [the longest x2 16.3 us: gradient_of(): theirs = lax.ppermute(product(other).astype(BF16), 'c', swap)]
  transfers between devices with their start and end apart: 4 -> 7, of which waited for: 4 -> 5; matrix products, arithmetic and copies ran while one was open for 0% -> 3% of each run, Pallas kernels for 0% -> 0%
where the time goes in v1:
time: 250 us; the launch traced here: 246 us
  blocking collectives  110 us (44%)
  starting transfers between devices  53.5 us (21%)
  waiting for transfers between devices  53.5 us (21%)
  matrix products  10.9 us (4%)
  local copies, waits for them, and re-layouts  5.44 us (2%)
  Pallas kernels  4.51 us (2%)
  other arithmetic  4.39 us (2%)
  between operations  4.23 us (2%)
    all_gather x2, blocking collectives, gradient_of(): grads = lax.all_gather(grads, 'mp', axis=0, tiled=True)  41.1 us
    all_to_all x1, blocking collectives, local(): received = lax.all_to_all(sent, 'mp', 0, 0)  27.4 us
    all_to_all x1, waiting for transfers between devices, local(): lax.all_to_all(queries_of(*pair), 'mp', 0, 0)  22.1 us
    all_to_all x1, blocking collectives, gather_rows(): own = lax.all_to_all(block, 'q', 0, 0)  22 us
    all_to_all x1, blocking collectives, gradient_of(): received = lax.all_to_all(summed.reshape(groups, PAD, width), 'q', 0, 0)  19.1 us
    ppermute x2, starting transfers between devices, gradient_of(): theirs = lax.ppermute(product(other).astype(BF16), 'c', swap)  16.3 us
    all_to_all x1, waiting for transfers between devices, gather_rows(): own = lax.all_to_all(block, 'q', 0, 0)  14.3 us
    all_to_all x1, waiting for transfers between devices, gradient_of(): received = lax.all_to_all(summed.reshape(groups, PAD, width), 'q', 0, 0)  14.1 us
  transfers between devices with their start and end apart: 7, of which 5 were waited for; matrix products, arithmetic and copies ran while one was open for 3% of the time, Pallas kernels for 0%

profile of v1, /device:TPU:1, one launch (start us, length us, event | category | flops | bytes accessed | tf_op | source)
XLA Modules:
  0.0 246.1 jit_solution(12159037989699338454)
XLA Ops:
  2.4 10.5 %all-to-all-start = ((bf16[32,16,512]{2,1,0:T(8,128)(2,1)}), bf16[32,16,512]{2,1,0:T(8,128)(2,1)S(1)}, u32[]{:S(2)}, u32[]{:S(2)}) async-start(bf16[32,16,512]{2,1,0:T(8,128)(2,1)} %broadcast_in_dim.64), calls=%async_computation | async-start | bytes 1048576 | tf_op jit(solution)/shard_map/all_to_all | solution.py:103
  12.9 14.3 %all-to-all-done = bf16[32,16,512]{2,1,0:T(8,128)(2,1)S(1)} async-done(((bf16[32,16,512]{2,1,0:T(8,128)(2,1)}), bf16[32,16,512]{2,1,0:T(8,128)(2,1)S(1)}, u32[]{:S(2)}, u32[]{:S(2)}) %all-to-all-start) | async-done | bytes 524320 | tf_op jit(solution)/shard_map/all_to_all | solution.py:103
  27.2 5.4 %collective-permute-start = (bf16[32,16,512]{2,1,0:T(8,128)(2,1)S(1)}, bf16[32,16,512]{2,1,0:T(8,128)(2,1)S(1)}, u32[]{:S(2)}, u32[]{:S(2)}) collective-permute-start(bf16[32,16,512]{2,1,0:T(8,128)(2,1)S(1)} %all-to-all-done), channel_id=1, source_target_pairs={{0,8},{8,0},{1,9},{9,1},{2,10},{10,2},{3,11},{11,3},{4,12},{12,4},... | collective-permute-start | bytes 1572872 | tf_op jit(solution)/shard_map/ppermute | solution.py:104
  32.6 1.8 fusion.25
  35.0 1.5 add_convert_fusion.1
  36.5 10.0 %all-to-all-start.1 = ((bf16[8,96,512]{2,1,0:T(8,128)(2,1)}), bf16[8,96,512]{2,1,0:T(8,128)(2,1)S(1)}, u32[]{:S(2)}, u32[]{:S(2)}) async-start(bf16[8,96,512]{2,1,0:T(8,128)(2,1)} %bitcast.3), calls=%async_computation.1 | async-start | bytes 1572864 | tf_op jit(solution)/shard_map/all_to_all | solution.py:126
  46.5 1.5 constant_dynamic-slice_fusion.cotangent_ref
  48.1 22.1 %all-to-all-done.1.partial_ref = bf16[8,96,512]{2,1,0:T(8,128)(2,1)S(1)} async-done(((bf16[8,96,512]{2,1,0:T(8,128)(2,1)}), bf16[8,96,512]{2,1,0:T(8,128)(2,1)S(1)}, u32[]{:S(2)}, u32[]{:S(2)}) %all-to-all-start.1) | async-done | bytes 786464 | tf_op jit(solution)/shard_map/all_to_all | solution.py:126
  71.1 2.2 head_grad.2
  73.4 20.6 %all_gather.6 = bf16[768,512]{1,0:T(8,128)(2,1)S(1)} all-gather(bf16[96,512]{1,0:T(8,128)(2,1)} %get-tuple-element.6), channel_id=1, replica_groups=mesh['q'=32,'c'=2,'mp'=8] {'mp'}, dimensions={0}, use_global_device_ids=true | all-gather | bytes 884736 | tf_op jit(solution)/shard_map/all_gather | solution.py:112
  94.6 8.1 %collective-permute-start.1 = (bf16[512,512]{1,0:T(8,128)(2,1)S(1)}, bf16[512,512]{1,0:T(8,128)(2,1)S(1)}, u32[]{:S(2)}, u32[]{:S(2)}) collective-permute-start(bf16[512,512]{1,0:T(8,128)(2,1)S(1)} %convolution_convert_fusion.2), channel_id=1, source_target_pairs={{0,8},{8,0},{1,9},{9,1},{2,10},{10,2},{3,11},{11,3},{4,12},{12,4},... | collective-permute-start | bytes 1572872 | tf_op jit(solution)/shard_map/ppermute | solution.py:117
  102.7 1.5 collective-permute-done.1
  105.6 5.3 %all-to-all-start.2 = ((bf16[32,16,512]{2,1,0:T(8,128)(2,1)}), bf16[32,16,512]{2,1,0:T(8,128)(2,1)S(1)}, u32[]{:S(2)}, u32[]{:S(2)}) async-start(bf16[32,16,512]{2,1,0:T(8,128)(2,1)} %bitcast.24), calls=%async_computation.2 | async-start | bytes 1048576 | tf_op jit(solution)/shard_map/all_to_all | solution.py:119
  110.9 14.1 %all-to-all-done.2 = bf16[32,16,512]{2,1,0:T(8,128)(2,1)S(1)} async-done(((bf16[32,16,512]{2,1,0:T(8,128)(2,1)}), bf16[32,16,512]{2,1,0:T(8,128)(2,1)S(1)}, u32[]{:S(2)}, u32[]{:S(2)}) %all-to-all-start.2) | async-done | bytes 524320 | tf_op jit(solution)/shard_map/all_to_all | solution.py:119
  127.2 22.0 %all_to_all.30 = bf16[32,16,512]{2,1,0:T(8,128)(2,1)S(1)} all-to-all(bf16[32,16,512]{2,1,0:T(8,128)(2,1)S(1)} %broadcast_in_dim.71), channel_id=1, replica_groups=mesh['q'=32,'c'=2,'mp'=8] {'q'}, dimensions={0} | all-to-all | bytes 1048576 | tf_op jit(solution)/shard_map/all_to_all | solution.py:103
  149.2 5.9 %collective-permute-start.2 = (bf16[32,16,512]{2,1,0:T(8,128)(2,1)S(1)}, bf16[32,16,512]{2,1,0:T(8,128)(2,1)}, u32[]{:S(2)}, u32[]{:S(2)}) collective-permute-start(bf16[32,16,512]{2,1,0:T(8,128)(2,1)S(1)} %all_to_all.30), channel_id=1, source_target_pairs={{0,8},{8,0},{1,9},{9,1},{2,10},{10,2},{3,11},{11,3},{4,12},{12,4},... | collective-permute-start | bytes 1572872 | tf_op jit(solution)/shard_map/ppermute | solution.py:104
  155.9 1.8 fusion.32
  160.6 2.2 add_convert_fusion
  162.9 27.4 %all_to_all.31.partial_ref = bf16[8,104,512]{2,1,0:T(8,128)(2,1)S(1)} all-to-all(bf16[8,104,512]{2,1,0:T(8,128)(2,1)S(1)} %pad_maximum_fusion), channel_id=1, replica_groups=mesh['q'=32,'c'=2,'mp'=8] {'mp'}, dimensions={0} | all-to-all | bytes 1703936 | tf_op jit(solution)/shard_map/all_to_all | solution.py:139
  192.5 2.3 head_grad.3
  194.8 20.5 %all_gather.7 = bf16[768,512]{1,0:T(8,128)(2,1)S(1)} all-gather(bf16[96,512]{1,0:T(8,128)(2,1)} %get-tuple-element.8), channel_id=1, replica_groups=mesh['q'=32,'c'=2,'mp'=8] {'mp'}, dimensions={0}, use_global_device_ids=true | all-gather | bytes 884736 | tf_op jit(solution)/shard_map/all_gather | solution.py:112
  215.9 8.3 %collective-permute-start.3 = (bf16[512,512]{1,0:T(8,128)(2,1)S(1)}, bf16[512,512]{1,0:T(8,128)(2,1)S(1)}, u32[]{:S(2)}, u32[]{:S(2)}) collective-permute-start(bf16[512,512]{1,0:T(8,128)(2,1)S(1)} %convolution_convert_fusion.1), channel_id=1, source_target_pairs={{0,8},{8,0},{1,9},{9,1},{2,10},{10,2},{3,11},{11,3},{4,12},{12,4},... | collective-permute-start | bytes 1572872 | tf_op jit(solution)/shard_map/ppermute | solution.py:117
  224.1 1.5 collective-permute-done.3
  226.2 19.1 %all_to_all.32 = bf16[32,16,512]{2,1,0:T(8,128)(2,1)S(1)} all-to-all(bf16[32,16,512]{2,1,0:T(8,128)(2,1)S(1)} %bitcast.25), channel_id=1, replica_groups=mesh['q'=32,'c'=2,'mp'=8] {'q'}, dimensions={0} | all-to-all | bytes 1048576 | tf_op jit(solution)/shard_map/all_to_all | solution.py:119
  (47 shorter events, 12.0 us)
Async XLA Ops:
  0.6 32.0 %copy-start = (bf16[768,768]{1,0:T(8,128)(2,1)S(1)}, bf16[768,768]{1,0:T(8,128)(2,1)}, u32[]{:S(2)}) copy-start(bf16[768,768]{1,0:T(8,128)(2,1)} %param.5) | copy-start | bytes 3538948
  2.4 24.8 %all-to-all-start = ((bf16[32,16,512]{2,1,0:T(8,128)(2,1)}), bf16[32,16,512]{2,1,0:T(8,128)(2,1)S(1)}, u32[]{:S(2)}, u32[]{:S(2)}) async-start(bf16[32,16,512]{2,1,0:T(8,128)(2,1)} %broadcast_in_dim.64), calls=%async_computation | async-start | bytes 1048576 | tf_op jit(solution)/shard_map/all_to_all | solution.py:103
  27.2 7.8 %collective-permute-start = (bf16[32,16,512]{2,1,0:T(8,128)(2,1)S(1)}, bf16[32,16,512]{2,1,0:T(8,128)(2,1)S(1)}, u32[]{:S(2)}, u32[]{:S(2)}) collective-permute-start(bf16[32,16,512]{2,1,0:T(8,128)(2,1)S(1)} %all-to-all-done), channel_id=1, source_target_pairs={{0,8},{8,0},{1,9},{9,1},{2,10},{10,2},{3,11},{11,3},{4,12},{12,4},... | collective-permute-start | bytes 1572872 | tf_op jit(solution)/shard_map/ppermute | solution.py:104
  36.5 33.7 %all-to-all-start.1 = ((bf16[8,96,512]{2,1,0:T(8,128)(2,1)}), bf16[8,96,512]{2,1,0:T(8,128)(2,1)S(1)}, u32[]{:S(2)}, u32[]{:S(2)}) async-start(bf16[8,96,512]{2,1,0:T(8,128)(2,1)} %bitcast.3), calls=%async_computation.1 | async-start | bytes 1572864 | tf_op jit(solution)/shard_map/all_to_all | solution.py:126
  70.2 1.0 copy-start.2
  94.6 9.6 %collective-permute-start.1 = (bf16[512,512]{1,0:T(8,128)(2,1)S(1)}, bf16[512,512]{1,0:T(8,128)(2,1)S(1)}, u32[]{:S(2)}, u32[]{:S(2)}) collective-permute-start(bf16[512,512]{1,0:T(8,128)(2,1)S(1)} %convolution_convert_fusion.2), channel_id=1, source_target_pairs={{0,8},{8,0},{1,9},{9,1},{2,10},{10,2},{3,11},{11,3},{4,12},{12,4},... | collective-permute-start | bytes 1572872 | tf_op jit(solution)/shard_map/ppermute | solution.py:117
  105.6 19.5 %all-to-all-start.2 = ((bf16[32,16,512]{2,1,0:T(8,128)(2,1)}), bf16[32,16,512]{2,1,0:T(8,128)(2,1)S(1)}, u32[]{:S(2)}, u32[]{:S(2)}) async-start(bf16[32,16,512]{2,1,0:T(8,128)(2,1)} %bitcast.24), calls=%async_computation.2 | async-start | bytes 1048576 | tf_op jit(solution)/shard_map/all_to_all | solution.py:119
  149.2 8.5 %collective-permute-start.2 = (bf16[32,16,512]{2,1,0:T(8,128)(2,1)S(1)}, bf16[32,16,512]{2,1,0:T(8,128)(2,1)}, u32[]{:S(2)}, u32[]{:S(2)}) collective-permute-start(bf16[32,16,512]{2,1,0:T(8,128)(2,1)S(1)} %all_to_all.30), channel_id=1, source_target_pairs={{0,8},{8,0},{1,9},{9,1},{2,10},{10,2},{3,11},{11,3},{4,12},{12,4},... | collective-permute-start | bytes 1572872 | tf_op jit(solution)/shard_map/ppermute | solution.py:104
  190.3 0.9 copy-start.1
  215.9 9.8 %collective-permute-start.3 = (bf16[512,512]{1,0:T(8,128)(2,1)S(1)}, bf16[512,512]{1,0:T(8,128)(2,1)S(1)}, u32[]{:S(2)}, u32[]{:S(2)}) collective-permute-start(bf16[512,512]{1,0:T(8,128)(2,1)S(1)} %convolution_convert_fusion.1), channel_id=1, source_target_pairs={{0,8},{8,0},{1,9},{9,1},{2,10},{10,2},{3,11},{11,3},{4,12},{12,4},... | collective-permute-start | bytes 1572872 | tf_op jit(solution)/shard_map/ppermute | solution.py:117
  226.2 19.2 %copy-start.3 = (f32[12,512]{1,0:T(8,128)S(1)}, f32[12,512]{1,0:T(8,128)}, u32[]{:S(2)}) copy-start(f32[12,512]{1,0:T(8,128)} %param.7) | copy-start | bytes 73732
  226.2 19.2 %copy-start.4 = (f32[12,512]{1,0:T(8,128)S(1)}, f32[12,512]{1,0:T(8,128)}, u32[]{:S(2)}) copy-start(f32[12,512]{1,0:T(8,128)} %param.8) | copy-start | bytes 73732
  226.2 19.2 %copy-start.5 = (f32[12,512]{1,0:T(8,128)S(1)}, f32[12,512]{1,0:T(8,128)}, u32[]{:S(2)}) copy-start(f32[12,512]{1,0:T(8,128)} %param.9) | copy-start | bytes 73732

commit v2 on v1

v2 whole, which is shorter than its diff:
```python
import functools
import math

import jax
import jax.numpy as jnp
from jax import lax
from jax.experimental import pallas as pl
from jax.experimental.pallas import tpu as pltpu
from jax.sharding import Mesh
from jax.sharding import PartitionSpec as P

HEAD_DIM = 128
PAD = 16
TAIL = 8
CORES = 2
MP = ("far", "near")
VMEM_BYTES = 16 * 1024 * 1024

radius = 8.0
rate = 0.005
decay_one = 0.9
decay_two = 0.95
weight_decay = 0.1
step_count = 10

BF16 = jnp.bfloat16
F32 = jnp.float32


def pieces_of(value, shape, row):
    high = value.astype(BF16).astype(F32)
    rest = value - high
    middle = rest.astype(BF16).astype(F32)
    low = rest - middle
    rows = lax.broadcasted_iota(jnp.int32, shape, len(shape) - 2)
    lanes = lax.broadcasted_iota(jnp.int32, shape, len(shape) - 1)
    picked = jnp.where(lanes == 0, high, jnp.where(lanes == 1, middle, jnp.where(lanes == 2, low, 0.0)))
    return jnp.where(rows == row, picked, 0.0)


def scalar_in(block, row):
    rows = lax.broadcasted_iota(jnp.int32, block.shape, len(block.shape) - 2)
    lanes = lax.broadcasted_iota(jnp.int32, block.shape, len(block.shape) - 1)
    return jnp.sum(jnp.where((rows == row) & (lanes < 3), block.astype(F32), 0.0))


def call(kernel, name, out_shape, *operands, cost=(0, 0)):
    vmem = pl.BlockSpec(memory_space=pltpu.VMEM)
    return pl.pallas_call(
        kernel,
        in_specs=[vmem] * len(operands),
        out_specs=jax.tree.map(lambda _: vmem, out_shape),
        out_shape=out_shape,
        compiler_params=pltpu.CompilerParams(vmem_limit_bytes=VMEM_BYTES),
        cost_estimate=pl.CostEstimate(flops=cost[0], bytes_accessed=cost[1], transcendentals=0),
        name=name,
    )(*operands)


def head_kernel(second, partial_ref, *refs):
    base_ref = refs[0] if second else None
    cotangent_ref = refs[1] if second else refs[0]
    out_ref = refs[-1]
    tokens, width = cotangent_ref.shape
    if second:
        squares = scalar_in(partial_ref[:, tokens : tokens + TAIL, 0:HEAD_DIM], 0)
        scale = radius * lax.rsqrt(jnp.full((1, HEAD_DIM), squares + 1e-06, F32))
    for head in range(width // HEAD_DIM):
        lanes = slice(head * HEAD_DIM, (head + 1) * HEAD_DIM)
        queries = partial_ref[0, 0:tokens, lanes].astype(F32)
        for part in range(1, partial_ref.shape[0]):
            queries = queries + partial_ref[part, 0:tokens, lanes].astype(F32)
        if second:
            queries = queries * scale + base_ref[:, lanes]
        else:
            refs[-2][:, lanes] = queries
        cotangent = cotangent_ref[:, lanes].astype(F32)
        centred = queries - jnp.mean(queries, axis=-1, keepdims=True)
        spread = jnp.mean(centred * centred, axis=-1, keepdims=True)
        factor = lax.rsqrt(spread + 1e-06)
        normed = centred * factor
        level = jnp.mean(cotangent, axis=-1, keepdims=True)
        along = jnp.mean(cotangent * normed, axis=-1, keepdims=True)
        out_ref[:, lanes] = (factor * (cotangent - level - normed * along)).astype(BF16)


def spread_kernel(weights_ref, out_ref):
    rows, width = weights_ref.shape
    out_ref[...] = jnp.zeros(out_ref.shape, BF16)
    block = weights_ref[...].astype(BF16)
    for part in range(out_ref.shape[0]):
        out_ref[part, 0:rows, :] = block


def pack_kernel(rows, loss_scale, received_ref, out_ref):
    total = received_ref[0].astype(F32)
    for part in range(1, received_ref.shape[0]):
        total = total + received_ref[part].astype(F32)
    total = total * loss_scale
    block = (total + pieces_of(jnp.sum(total * total), total.shape, rows)).astype(BF16)
    for part in range(out_ref.shape[0]):
        out_ref[part] = block


def change_kernel(rows, tokens_ref, own_ref, theirs_ref, value_ref, out_ref):
    parts, share, width = out_ref.shape
    share = share - TAIL
    squares = scalar_in(own_ref[:, :, 0:HEAD_DIM], rows) + scalar_in(theirs_ref[:, :, 0:HEAD_DIM], rows)
    tail = pieces_of(squares, (TAIL, width), 0).astype(BF16)
    first = theirs_ref[...].reshape(-1, width)
    step = parts // 2
    for side in range(2):
        picked = slice(side * step * share, (side + 1) * step * share)
        value = value_ref[picked, :] + jnp.dot(
            tokens_ref[picked, first.shape[0] :], first, preferred_element_type=F32
        )
        for part in range(step):
            out_ref[side * step + part, 0:share, :] = value[part * share : (part + 1) * share].astype(BF16)
            out_ref[side * step + part, share : share + TAIL, :] = tail


def local(tokens, cotangent, weights, moment_one, moment_two):
    count, depth = tokens.shape
    rows, columns = weights.shape
    groups = lax.axis_size("q")
    parts = lax.axis_size(MP)
    loss_scale = 1.0 / math.sqrt(count * groups * CORES)
    core = lax.axis_index("c")
    share = count // parts
    half = groups * PAD
    shape = jax.ShapeDtypeStruct

    feature = lax.broadcasted_iota(jnp.int32, (depth, CORES * half), 0)
    slot = lax.broadcasted_iota(jnp.int32, (depth, CORES * half), 1)
    place = slot % half
    source = jnp.where(slot < half, core, 1 - core)
    target = ((place // PAD) * CORES + source) * rows + place % PAD
    choose = ((feature == target) & (place % PAD < rows)).astype(BF16)
    spread_tokens = jnp.dot(tokens, choose, preferred_element_type=F32).astype(BF16)
    mine, other = spread_tokens[:, :half], spread_tokens[:, half:]

    cot = lax.dynamic_slice_in_dim(cotangent, lax.axis_index(MP) * share, share, 0)
    swap = [(0, 1), (1, 0)]

    def gather_rows(blocks):
        own = lax.all_to_all(blocks, "q", 0, 0)
        theirs = lax.ppermute(own, "c", swap)
        value = jnp.dot(mine, own.reshape(half, columns), preferred_element_type=F32)
        return own, theirs, value

    def gradient_of(grads):
        grads = lax.all_gather(grads, "near", axis=0, tiled=True)
        grads = lax.all_gather(grads, "far", axis=0, tiled=True)

        def product(side):
            return lax.dot_general(side, grads, (((0,), (0,)), ((), ())), preferred_element_type=F32)

        theirs = lax.ppermute(product(other).astype(BF16), "c", swap)
        summed = (product(mine) + theirs.astype(F32)).astype(BF16)
        return lax.all_to_all(summed.reshape(groups, PAD, columns), "q", 0, 0)

    blocks = shape((groups, PAD, columns), BF16)
    _, theirs, value = gather_rows(call(spread_kernel, "spread", blocks, weights))
    sent = value + jnp.dot(other, theirs.reshape(half, columns), preferred_element_type=F32)
    received = lax.all_to_all(sent.astype(BF16).reshape(parts, share, columns), MP, 0, 0)
    outs = (shape((share, columns), F32), shape((share, columns), BF16))
    queries, grads = call(functools.partial(head_kernel, False), "first_heads", outs, received, cot)
    received = gradient_of(grads)

    packed = call(functools.partial(pack_kernel, rows, loss_scale), "pack", blocks, received)
    own, theirs, value = gather_rows(packed)
    sent = call(
        functools.partial(change_kernel, rows),
        "change",
        shape((parts, share + TAIL, columns), BF16),
        spread_tokens,
        own,
        theirs,
        value,
        cost=(2 * count * half * columns, 8 * count * columns),
    )
    received = lax.all_to_all(sent, MP, 0, 0)
    grads = call(functools.partial(head_kernel, True), "second_heads", outs[1], received, queries, cot)
    received = gradient_of(grads)
    second = (jnp.sum(received.astype(F32), axis=0) * loss_scale)[:rows]

    new_moment_one = decay_one * moment_one + (1.0 - decay_one) * second
    new_moment_two = decay_two * moment_two + (1.0 - decay_two) * second * second
    correct_one = 1.0 - decay_one**step_count
    correct_two = 1.0 - decay_two**step_count
    update = new_moment_one / correct_one / (jnp.sqrt(new_moment_two / correct_two) + 1e-08)
    new_weights = weights - rate * (update + weight_decay * weights)
    return (new_weights, new_moment_one, new_moment_two)


def solution(mesh):
    groups = mesh.shape["dp"] // CORES
    far = mesh.shape["mp"] // 2
    fine = Mesh(mesh.devices.reshape(groups, CORES, far, 2), ("q", "c") + MP)
    dp = ("q", "c")
    shard = P(MP + dp, None)
    in_specs = (P(dp, MP), P(dp, None), shard, shard, shard)
    return jax.shard_map(local, mesh=fine, in_specs=in_specs, out_specs=(shard, shard, shard), check_vma=False)
```

time: 250 us -> 232 us (0.928)
  blocking collectives: 110 us -> 127 us
  waiting for transfers between devices: 53.5 us -> 40.3 us
  starting transfers between devices: 53.5 us -> 46.5 us
  matrix products: 10.9 us -> 6.81 us
  other arithmetic: 4.39 us -> 0.75 us
  between operations: 4.23 us -> 0.85 us
    all_to_all x3 -> x4, blocking collectives: 68.5 us -> 87.9 us  [the longest x2 38.4 us: gradient_of(): return lax.all_to_all(summed.reshape(groups, PAD, columns), 'q', 0, 0)]
    all_to_all x3 -> x2, waiting for transfers between devices: 50.5 us -> 36.4 us  [the longest x1 22.1 us: local(): lax.all_to_all(sent.astype(BF16).reshape(parts, share, columns), MP, 0, 0)]
    all_to_all x3 -> x2, starting transfers between devices: 25.9 us -> 20.5 us  [the longest x1 10.5 us: gather_rows(): own = lax.all_to_all(blocks, 'q', 0, 0)]
    dot_general x4 -> x3, matrix products: 6.03 us -> 2.65 us  [the longest x1 1.49 us: local(): jnp.dot(other, theirs.reshape(half, columns), preferred_element_type=F32)]
    reduce_sum x6 -> x1, other arithmetic: 2.6 us -> 0.08 us  [local(): second = (jnp.sum(received.astype(F32), axis=0) * loss_scale)[:rows]]
    all_gather x2 -> x4, blocking collectives: 41.1 us -> 39.5 us  [the longest x2 30.8 us: gradient_of(): grads = lax.all_gather(grads, 'far', axis=0, tiled=True)]
  transfers between devices with their start and end apart: 7 -> 6, of which waited for: 5 -> 5; matrix products, arithmetic and copies ran while one was open for 3% -> 2% of each run, Pallas kernels for 0% -> 0%
where the time goes in v2:
time: 232 us; the launch traced here: 228 us
  blocking collectives  127 us (55%)
  starting transfers between devices  46.5 us (20%)
  waiting for transfers between devices  40.3 us (17%)
  matrix products  6.81 us (3%)
  local copies, waits for them, and re-layouts  3.32 us (1%)
  Pallas kernels  2.45 us (1%)
    all_to_all x2, blocking collectives, gradient_of(): return lax.all_to_all(summed.reshape(groups, PAD, columns), 'q', 0, 0)  38.4 us
    all_gather x2, blocking collectives, gradient_of(): grads = lax.all_gather(grads, 'far', axis=0, tiled=True)  30.8 us
    all_to_all x1, blocking collectives, local(): received = lax.all_to_all(sent, MP, 0, 0)  27.6 us
    all_to_all x1, waiting for transfers between devices, local(): lax.all_to_all(sent.astype(BF16).reshape(parts, share, columns), MP, 0, 0)  22.1 us
    all_to_all x1, blocking collectives, gather_rows(): own = lax.all_to_all(blocks, 'q', 0, 0)  22 us
    ppermute x2, starting transfers between devices, gradient_of(): theirs = lax.ppermute(product(other).astype(BF16), 'c', swap)  14.7 us
    all_to_all x1, waiting for transfers between devices, gather_rows(): own = lax.all_to_all(blocks, 'q', 0, 0)  14.3 us
    ppermute x2, starting transfers between devices, gather_rows(): theirs = lax.ppermute(own, 'c', swap)  11.3 us
  transfers between devices with their start and end apart: 6, of which 5 were waited for; matrix products, arithmetic and copies ran while one was open for 2% of the time, Pallas kernels for 0%

profile of v2, /device:TPU:1, one launch (start us, length us, event | category | flops | bytes accessed | tf_op | source)
XLA Modules:
  0.0 228.5 jit_solution(8375093343640929785)
XLA Ops:
  1.5 0.9 spread.1
  2.4 10.5 %all-to-all-start = ((bf16[32,16,512]{2,1,0:T(8,128)(2,1)}), bf16[32,16,512]{2,1,0:T(8,128)(2,1)S(1)}, u32[]{:S(2)}, u32[]{:S(2)}) async-start(bf16[32,16,512]{2,1,0:T(8,128)(2,1)} %spread.1), calls=%async_computation | async-start | bytes 1048576 | tf_op jit(solution)/shard_map/all_to_all | solution.py:146
  12.9 14.3 %all-to-all-done = bf16[32,16,512]{2,1,0:T(8,128)(2,1)S(1)} async-done(((bf16[32,16,512]{2,1,0:T(8,128)(2,1)}), bf16[32,16,512]{2,1,0:T(8,128)(2,1)S(1)}, u32[]{:S(2)}, u32[]{:S(2)}) %all-to-all-start) | async-done | bytes 524320 | tf_op jit(solution)/shard_map/all_to_all | solution.py:146
  27.2 5.4 %collective-permute-start = (bf16[32,16,512]{2,1,0:T(8,128)(2,1)S(1)}, bf16[32,16,512]{2,1,0:T(8,128)(2,1)S(1)}, u32[]{:S(2)}, u32[]{:S(2)}) collective-permute-start(bf16[32,16,512]{2,1,0:T(8,128)(2,1)S(1)} %all-to-all-done), channel_id=1, source_target_pairs={{0,8},{8,0},{1,9},{9,1},{2,10},{10,2},{3,11},{11,3},{4,12},{12,4},... | collective-permute-start | bytes 1572872 | tf_op jit(solution)/shard_map/ppermute | solution.py:147
  32.6 1.7 fusion.29.tokens_ref
  34.9 1.5 add_convert_fusion
  36.4 10.0 %all-to-all-start.1 = ((bf16[8,96,512]{2,1,0:T(8,128)(2,1)}), bf16[8,96,512]{2,1,0:T(8,128)(2,1)S(1)}, u32[]{:S(2)}, u32[]{:S(2)}) async-start(bf16[8,96,512]{2,1,0:T(8,128)(2,1)} %bitcast.17), calls=%async_computation.1 | async-start | bytes 1572864 | tf_op jit(solution)/shard_map/all_to_all | solution.py:165
  46.5 1.5 constant_dynamic-slice_fusion.refs_0_.refs_1_
  48.0 22.1 %all-to-all-done.1.partial_ref = bf16[8,96,512]{2,1,0:T(8,128)(2,1)S(1)} async-done(((bf16[8,96,512]{2,1,0:T(8,128)(2,1)}), bf16[8,96,512]{2,1,0:T(8,128)(2,1)S(1)}, u32[]{:S(2)}, u32[]{:S(2)}) %all-to-all-start.1) | async-done | bytes 786464 | tf_op jit(solution)/shard_map/all_to_all | solution.py:165
  70.1 0.9 copy-done.1
  71.4 4.6 %all_gather.12 = bf16[192,512]{1,0:T(8,128)(2,1)S(1)} all-gather(bf16[96,512]{1,0:T(8,128)(2,1)S(1)} %get-tuple-element.5), channel_id=1, replica_groups=mesh['q'=32,'c'=2,'far'=4,'near'=2] {'near'}, dimensions={0}, use_global_device_ids=true | all-gather | bytes 294912 | tf_op jit(solution)/shard_map/all_gather | solution.py:152
  76.0 15.1 %all_gather.13 = bf16[768,512]{1,0:T(8,128)(2,1)S(1)} all-gather(bf16[192,512]{1,0:T(8,128)(2,1)S(1)} %all_gather.12), channel_id=1, replica_groups=mesh['q'=32,'c'=2,'far'=4,'near'=2] {'far'}, dimensions={0}, use_global_device_ids=true | all-gather | bytes 983040 | tf_op jit(solution)/shard_map/all_gather | solution.py:153
  91.7 7.9 %collective-permute-start.1 = (bf16[512,512]{1,0:T(8,128)(2,1)S(1)}, bf16[512,512]{1,0:T(8,128)(2,1)S(1)}, u32[]{:S(2)}, u32[]{:S(2)}) collective-permute-start(bf16[512,512]{1,0:T(8,128)(2,1)S(1)} %convolution_convert_fusion.1), channel_id=1, source_target_pairs={{0,8},{8,0},{1,9},{9,1},{2,10},{10,2},{3,11},{11,3},{4,12},{12,4},... | collective-permute-start | bytes 1572872 | tf_op jit(solution)/shard_map/ppermute | solution.py:158
  99.6 1.5 collective-permute-done.1
  101.7 19.3 %all_to_all.30.received_ref = bf16[32,16,512]{2,1,0:T(8,128)(2,1)S(1)} all-to-all(bf16[32,16,512]{2,1,0:T(8,128)(2,1)S(1)} %bitcast.21), channel_id=1, replica_groups=mesh['q'=32,'c'=2,'far'=4,'near'=2] {'q'}, dimensions={0} | all-to-all | bytes 1048576 | tf_op jit(solution)/shard_map/all_to_all | solution.py:160
  121.2 22.0 %all_to_all.31.own_ref = bf16[32,16,512]{2,1,0:T(8,128)(2,1)S(1)} all-to-all(bf16[32,16,512]{2,1,0:T(8,128)(2,1)S(1)} %pack.1), channel_id=1, replica_groups=mesh['q'=32,'c'=2,'far'=4,'near'=2] {'q'}, dimensions={0} | all-to-all | bytes 1048576 | tf_op jit(solution)/shard_map/all_to_all | solution.py:146
  143.2 5.9 %collective-permute-start.2 = (bf16[32,16,512]{2,1,0:T(8,128)(2,1)S(1)}, bf16[32,16,512]{2,1,0:T(8,128)(2,1)S(1)}, u32[]{:S(2)}, u32[]{:S(2)}) collective-permute-start(bf16[32,16,512]{2,1,0:T(8,128)(2,1)S(1)} %all_to_all.31.own_ref), channel_id=1, source_target_pairs={{0,8},{8,0},{1,9},{9,1},{2,10},{10,2},{3,11},{11,3},{4,12},{12,4},... | collective-permute-start | bytes 1572872 | tf_op jit(solution)/shard_map/ppermute | solution.py:147
  149.7 0.9 collective-permute-done.2.theirs_ref
  151.2 27.6 %all_to_all.32.partial_ref = bf16[8,104,512]{2,1,0:T(8,128)(2,1)S(1)} all-to-all(bf16[8,104,512]{2,1,0:T(8,128)(2,1)S(1)} %change.1), channel_id=1, replica_groups=mesh['q'=32,'c'=2,'far'=4,'near'=2] {'far','near'}, dimensions={0} | all-to-all | bytes 1703936 | tf_op jit(solution)/shard_map/all_to_all | solution.py:182
  179.2 4.1 %all_gather.14 = bf16[192,512]{1,0:T(8,128)(2,1)S(1)} all-gather(bf16[96,512]{1,0:T(8,128)(2,1)S(1)} %second_heads.1), channel_id=1, replica_groups=mesh['q'=32,'c'=2,'far'=4,'near'=2] {'near'}, dimensions={0}, use_global_device_ids=true | all-gather | bytes 294912 | tf_op jit(solution)/shard_map/all_gather | solution.py:152
  183.4 15.6 %all_gather.15 = bf16[768,512]{1,0:T(8,128)(2,1)S(1)} all-gather(bf16[192,512]{1,0:T(8,128)(2,1)S(1)} %all_gather.14), channel_id=1, replica_groups=mesh['q'=32,'c'=2,'far'=4,'near'=2] {'far'}, dimensions={0}, use_global_device_ids=true | all-gather | bytes 983040 | tf_op jit(solution)/shard_map/all_gather | solution.py:153
  199.6 6.8 %collective-permute-start.3 = (bf16[512,512]{1,0:T(8,128)(2,1)S(1)}, bf16[512,512]{1,0:T(8,128)(2,1)S(1)}, u32[]{:S(2)}, u32[]{:S(2)}) collective-permute-start(bf16[512,512]{1,0:T(8,128)(2,1)S(1)} %convolution_convert_fusion), channel_id=1, source_target_pairs={{0,8},{8,0},{1,9},{9,1},{2,10},{10,2},{3,11},{11,3},{4,12},{12,4},... | collective-permute-start | bytes 1572872 | tf_op jit(solution)/shard_map/ppermute | solution.py:158
  206.4 1.5 collective-permute-done.3
  208.6 19.1 %all_to_all.33 = bf16[32,16,512]{2,1,0:T(8,128)(2,1)S(1)} all-to-all(bf16[32,16,512]{2,1,0:T(8,128)(2,1)S(1)} %bitcast.20), channel_id=1, replica_groups=mesh['q'=32,'c'=2,'far'=4,'near'=2] {'q'}, dimensions={0} | all-to-all | bytes 1048576 | tf_op jit(solution)/shard_map/all_to_all | solution.py:160
  (29 shorter events, 6.8 us)
Async XLA Ops:
  0.6 32.0 %copy-start = (bf16[768,768]{1,0:T(8,128)(2,1)S(1)}, bf16[768,768]{1,0:T(8,128)(2,1)}, u32[]{:S(2)}) copy-start(bf16[768,768]{1,0:T(8,128)(2,1)} %param.5) | copy-start | bytes 3538948
  0.6 0.9 copy-start.3
  2.4 24.8 %all-to-all-start = ((bf16[32,16,512]{2,1,0:T(8,128)(2,1)}), bf16[32,16,512]{2,1,0:T(8,128)(2,1)S(1)}, u32[]{:S(2)}, u32[]{:S(2)}) async-start(bf16[32,16,512]{2,1,0:T(8,128)(2,1)} %spread.1), calls=%async_computation | async-start | bytes 1048576 | tf_op jit(solution)/shard_map/all_to_all | solution.py:146
  27.2 7.7 %collective-permute-start = (bf16[32,16,512]{2,1,0:T(8,128)(2,1)S(1)}, bf16[32,16,512]{2,1,0:T(8,128)(2,1)S(1)}, u32[]{:S(2)}, u32[]{:S(2)}) collective-permute-start(bf16[32,16,512]{2,1,0:T(8,128)(2,1)S(1)} %all-to-all-done), channel_id=1, source_target_pairs={{0,8},{8,0},{1,9},{9,1},{2,10},{10,2},{3,11},{11,3},{4,12},{12,4},... | collective-permute-start | bytes 1572872 | tf_op jit(solution)/shard_map/ppermute | solution.py:147
  36.4 33.7 %all-to-all-start.1 = ((bf16[8,96,512]{2,1,0:T(8,128)(2,1)}), bf16[8,96,512]{2,1,0:T(8,128)(2,1)S(1)}, u32[]{:S(2)}, u32[]{:S(2)}) async-start(bf16[8,96,512]{2,1,0:T(8,128)(2,1)} %bitcast.17), calls=%async_computation.1 | async-start | bytes 1572864 | tf_op jit(solution)/shard_map/all_to_all | solution.py:165
  70.1 0.9 copy-start.1
  91.7 9.4 %collective-permute-start.1 = (bf16[512,512]{1,0:T(8,128)(2,1)S(1)}, bf16[512,512]{1,0:T(8,128)(2,1)S(1)}, u32[]{:S(2)}, u32[]{:S(2)}) collective-permute-start(bf16[512,512]{1,0:T(8,128)(2,1)S(1)} %convolution_convert_fusion.1), channel_id=1, source_target_pairs={{0,8},{8,0},{1,9},{9,1},{2,10},{10,2},{3,11},{11,3},{4,12},{12,4},... | collective-permute-start | bytes 1572872 | tf_op jit(solution)/shard_map/ppermute | solution.py:158
  143.2 7.4 %collective-permute-start.2 = (bf16[32,16,512]{2,1,0:T(8,128)(2,1)S(1)}, bf16[32,16,512]{2,1,0:T(8,128)(2,1)S(1)}, u32[]{:S(2)}, u32[]{:S(2)}) collective-permute-start(bf16[32,16,512]{2,1,0:T(8,128)(2,1)S(1)} %all_to_all.31.own_ref), channel_id=1, source_target_pairs={{0,8},{8,0},{1,9},{9,1},{2,10},{10,2},{3,11},{11,3},{4,12},{12,4},... | collective-permute-start | bytes 1572872 | tf_op jit(solution)/shard_map/ppermute | solution.py:147
  151.2 27.6 %copy-start.2 = (bf16[96,512]{1,0:T(8,128)(2,1)S(1)}, bf16[96,512]{1,0:T(8,128)(2,1)}, u32[]{:S(2)}) copy-start(bf16[96,512]{1,0:T(8,128)(2,1)} %constant_dynamic-slice_fusion.refs_0_.refs_1_) | copy-start | bytes 294916
  199.6 8.3 %collective-permute-start.3 = (bf16[512,512]{1,0:T(8,128)(2,1)S(1)}, bf16[512,512]{1,0:T(8,128)(2,1)S(1)}, u32[]{:S(2)}, u32[]{:S(2)}) collective-permute-start(bf16[512,512]{1,0:T(8,128)(2,1)S(1)} %convolution_convert_fusion), channel_id=1, source_target_pairs={{0,8},{8,0},{1,9},{9,1},{2,10},{10,2},{3,11},{11,3},{4,12},{12,4},... | collective-permute-start | bytes 1572872 | tf_op jit(solution)/shard_map/ppermute | solution.py:158
  208.5 19.2 %copy-start.4 = (f32[12,512]{1,0:T(8,128)S(1)}, f32[12,512]{1,0:T(8,128)}, u32[]{:S(2)}) copy-start(f32[12,512]{1,0:T(8,128)} %weights_ref.1) | copy-start | bytes 73732
  208.5 19.2 %copy-start.5 = (f32[12,512]{1,0:T(8,128)S(1)}, f32[12,512]{1,0:T(8,128)}, u32[]{:S(2)}) copy-start(f32[12,512]{1,0:T(8,128)} %param.8) | copy-start | bytes 73732
  208.6 19.2 %copy-start.6 = (f32[12,512]{1,0:T(8,128)S(1)}, f32[12,512]{1,0:T(8,128)}, u32[]{:S(2)}) copy-start(f32[12,512]{1,0:T(8,128)} %param.9) | copy-start | bytes 73732

commit v3 on v2

v3 whole, which is shorter than its diff:
```python
import functools
import math

import jax
import jax.numpy as jnp
from jax import lax
from jax.experimental import pallas as pl
from jax.experimental.pallas import tpu as pltpu
from jax.sharding import Mesh
from jax.sharding import PartitionSpec as P

HEAD_DIM = 128
TAIL = 8
CORES = 2
MP = ("far", "near")
VMEM_BYTES = 16 * 1024 * 1024

radius = 8.0
rate = 0.005
decay_one = 0.9
decay_two = 0.95
weight_decay = 0.1
step_count = 10

BF16 = jnp.bfloat16
F32 = jnp.float32


def pieces_of(value, shape, row):
    high = value.astype(BF16).astype(F32)
    rest = value - high
    middle = rest.astype(BF16).astype(F32)
    low = rest - middle
    rows = lax.broadcasted_iota(jnp.int32, shape, len(shape) - 2)
    lanes = lax.broadcasted_iota(jnp.int32, shape, len(shape) - 1)
    picked = jnp.where(lanes == 0, high, jnp.where(lanes == 1, middle, jnp.where(lanes == 2, low, 0.0)))
    return jnp.where(rows == row, picked, 0.0)


def scalar_in(block, row):
    rows = lax.broadcasted_iota(jnp.int32, block.shape, len(block.shape) - 2)
    lanes = lax.broadcasted_iota(jnp.int32, block.shape, len(block.shape) - 1)
    return jnp.sum(jnp.where((rows == row) & (lanes < 3), block.astype(F32), 0.0))


def call(kernel, name, out_shape, *operands, cost=(0, 0)):
    vmem = pl.BlockSpec(memory_space=pltpu.VMEM)
    smem = pl.BlockSpec(memory_space=pltpu.SMEM)
    return pl.pallas_call(
        kernel,
        in_specs=[smem if operand.dtype == jnp.int32 else vmem for operand in operands],
        out_specs=jax.tree.map(lambda _: vmem, out_shape),
        out_shape=out_shape,
        compiler_params=pltpu.CompilerParams(vmem_limit_bytes=VMEM_BYTES),
        cost_estimate=pl.CostEstimate(flops=cost[0], bytes_accessed=cost[1], transcendentals=0),
        name=name,
    )(*operands)


def head_kernel(second, partial_ref, *refs):
    base_ref = refs[0] if second else None
    cotangent_ref = refs[1] if second else refs[0]
    out_ref = refs[-1]
    tokens, width = cotangent_ref.shape
    if second:
        squares = scalar_in(partial_ref[:, tokens : tokens + TAIL, 0:HEAD_DIM], 0)
        scale = radius * lax.rsqrt(jnp.full((1, HEAD_DIM), squares + 1e-06, F32))
    for head in range(width // HEAD_DIM):
        lanes = slice(head * HEAD_DIM, (head + 1) * HEAD_DIM)
        queries = partial_ref[0, 0:tokens, lanes].astype(F32)
        for part in range(1, partial_ref.shape[0]):
            queries = queries + partial_ref[part, 0:tokens, lanes].astype(F32)
        if second:
            queries = queries * scale + base_ref[:, lanes]
        else:
            refs[-2][:, lanes] = queries
        cotangent = cotangent_ref[:, lanes].astype(F32)
        centred = queries - jnp.mean(queries, axis=-1, keepdims=True)
        spread = jnp.mean(centred * centred, axis=-1, keepdims=True)
        factor = lax.rsqrt(spread + 1e-06)
        normed = centred * factor
        level = jnp.mean(cotangent, axis=-1, keepdims=True)
        along = jnp.mean(cotangent * normed, axis=-1, keepdims=True)
        out_ref[:, lanes] = (factor * (cotangent - level - normed * along)).astype(BF16)


def swapped(core, one, two):
    return jnp.where(core == 0, one, two), jnp.where(core == 0, two, one)


def spread_kernel(core_ref, weights_ref, theirs_ref, out_ref):
    width = theirs_ref.shape[1]
    mine = swapped(core_ref[0, 0], weights_ref[:, :width], weights_ref[:, width:])[0]
    pair = swapped(core_ref[0, 0], mine, theirs_ref[...].astype(F32))
    block = jnp.concatenate(pair, axis=0).astype(BF16)
    for part in range(out_ref.shape[0]):
        out_ref[part] = block


def pack_kernel(loss_scale, received_ref, out_ref):
    total = received_ref[0].astype(F32)
    for part in range(1, received_ref.shape[0]):
        total = total + received_ref[part].astype(F32)
    block = (total * loss_scale).astype(BF16)
    for part in range(out_ref.shape[0]):
        out_ref[part] = block


def fold_kernel(loss_scale, core_ref, received_ref, kept_ref, given_ref):
    total = received_ref[0].astype(F32)
    for part in range(1, received_ref.shape[0]):
        total = total + received_ref[part].astype(F32)
    total = total * loss_scale
    rows = kept_ref.shape[0]
    kept_ref[...], given_ref[...] = swapped(core_ref[0, 0], total[:rows], total[rows:])


def update_kernel(core_ref, mine_ref, theirs_ref, weights_ref, one_ref, two_ref, *out_refs):
    width = mine_ref.shape[1]
    correct_one = 1.0 - decay_one**step_count
    correct_two = 1.0 - decay_two**step_count
    for side, second in enumerate(swapped(core_ref[0, 0], mine_ref[...], theirs_ref[...])):
        lanes = slice(side * width, (side + 1) * width)
        weights = weights_ref[:, lanes]
        new_one = decay_one * one_ref[:, lanes] + (1.0 - decay_one) * second
        new_two = decay_two * two_ref[:, lanes] + (1.0 - decay_two) * second * second
        update = new_one / correct_one / (jnp.sqrt(new_two / correct_two) + 1e-08)
        out_refs[0][:, lanes] = weights - rate * (update + weight_decay * weights)
        out_refs[1][:, lanes] = new_one
        out_refs[2][:, lanes] = new_two


def change_kernel(tokens_ref, first_ref, squares_ref, other_ref, out_ref):
    parts, share, width = out_ref.shape
    share = share - TAIL
    tail = pieces_of(squares_ref[...] + other_ref[...], (TAIL, width), 0).astype(BF16)
    step = 2
    for group in range(parts // step):
        picked = slice(group * step * share, (group + 1) * step * share)
        value = jnp.dot(tokens_ref[picked, :], first_ref[...], preferred_element_type=F32)
        for part in range(step):
            out_ref[group * step + part, 0:share, :] = value[part * share : (part + 1) * share].astype(BF16)
            out_ref[group * step + part, share : share + TAIL, :] = tail


def local(tokens, cotangent, weights, moment_one, moment_two):
    count, depth = tokens.shape
    rows, columns = weights.shape
    groups = lax.axis_size("q")
    parts = lax.axis_size(MP)
    loss_scale = 1.0 / math.sqrt(count * groups * CORES)
    core = lax.axis_index("c")
    share = count // parts
    width = columns // CORES
    shape = jax.ShapeDtypeStruct
    swap = [(0, 1), (1, 0)]

    which = core.reshape(1, 1).astype(jnp.int32)
    given = lax.dynamic_slice_in_dim(weights, (1 - core) * width, width, 1).astype(BF16)
    theirs = lax.ppermute(given, "c", swap)
    blocks = shape((groups, CORES * rows, width), BF16)
    spread = call(spread_kernel, "spread", blocks, which, weights, theirs)
    spread, tokens = lax.optimization_barrier((spread, tokens))

    theirs = lax.ppermute(tokens, "c", swap)
    pair = [side.reshape(parts, share, depth) for side in (tokens, theirs)]
    tokens = jnp.concatenate(pair, axis=1).reshape(-1, depth)

    cot = lax.dynamic_slice_in_dim(cotangent, lax.axis_index(MP) * share, share, 0)
    kept = lax.dynamic_slice_in_dim(cot, core * width, width, 1)
    given = lax.dynamic_slice_in_dim(cot, (1 - core) * width, width, 1)
    cot = jnp.concatenate([kept, lax.ppermute(given, "c", swap)], axis=0)

    def exchange(blocks):
        return lax.all_to_all(blocks, "q", 0, 0)

    def gradient_of(grads):
        grads = lax.all_gather(grads, "near", axis=0, tiled=True)
        grads = lax.all_gather(grads, "far", axis=0, tiled=True)
        summed = lax.dot_general(tokens, grads, (((0,), (0,)), ((), ())), preferred_element_type=F32)
        return exchange(summed.astype(BF16).reshape(groups, CORES * rows, width))

    gathered = exchange(spread)
    sent = jnp.dot(tokens, gathered.reshape(depth, width), preferred_element_type=F32)
    received = lax.all_to_all(sent.astype(BF16).reshape(parts, CORES * share, width), MP, 0, 0)
    outs = (shape((CORES * share, width), F32), shape((CORES * share, width), BF16))
    queries, grads = call(functools.partial(head_kernel, False), "first_heads", outs, received, cot)
    received = gradient_of(grads)

    packed = call(functools.partial(pack_kernel, loss_scale), "pack", blocks, received)
    first = exchange(packed).reshape(depth, width)
    squares = jnp.sum(jnp.square(first.astype(F32))).reshape(1, 1)
    sent = call(
        change_kernel,
        "change",
        shape((parts, CORES * share + TAIL, width), BF16),
        tokens,
        first,
        squares,
        lax.ppermute(squares, "c", swap),
        cost=(2 * CORES * count * depth * width, 2 * CORES * count * depth),
    )
    received = lax.all_to_all(sent, MP, 0, 0)
    grads = call(functools.partial(head_kernel, True), "second_heads", outs[1], received, queries, cot)
    half = shape((rows, width), F32)
    received = gradient_of(grads)
    mine, given = call(functools.partial(fold_kernel, loss_scale), "fold", (half, half), which, received)
    theirs = lax.ppermute(given, "c", swap)
    whole = shape((rows, columns), F32)
    return call(
        update_kernel, "update", (whole,) * 3, which, mine, theirs, weights, moment_one, moment_two
    )


def solution(mesh):
    groups = mesh.shape["dp"] // CORES
    far = mesh.shape["mp"] // 2
    fine = Mesh(mesh.devices.reshape(groups, CORES, far, 2), ("q", "c") + MP)
    dp = ("q", "c")
    shard = P(MP + dp, None)
    in_specs = (P(dp, MP), P(dp, None), shard, shard, shard)
    return jax.shard_map(local, mesh=fine, in_specs=in_specs, out_specs=(shard,) * 3, check_vma=False)
```

time: 232 us -> 212 us (0.914)
  waiting for transfers between devices: 40.3 us -> 28 us
  blocking collectives: 127 us -> 120 us
  matrix products: 6.81 us -> 4.32 us
    all_to_all x2, waiting for transfers between devices: 36.4 us -> 24.4 us  [the longest x1 13.7 us: local(): lax.all_to_all(sent.astype(BF16).reshape(parts, CORES * share, width), MP...]
    all_to_all x3, blocking collectives: 60.4 us -> 51.7 us  [exchange(): return lax.all_to_all(blocks, 'q', 0, 0)]
    ppermute x4 -> x5, starting transfers between devices: 26 us -> 34.4 us  [the longest x2 17.7 us: local(): theirs = lax.ppermute(given, 'c', swap)]
    all_to_all x2, starting transfers between devices: 20.5 us -> 14.4 us  [the longest x1 9.76 us: local(): lax.all_to_all(sent.astype(BF16).reshape(parts, CORES * share, width), MP...]
    dot_general x8 -> x3, matrix products: 6.81 us -> 4.32 us  [the longest x1 2.68 us: local(): jnp.dot(tokens, gathered.reshape(depth, width), preferred_element_type=F32)]
  transfers between devices with their start and end apart: 6 -> 7, of which waited for: 5 -> 6; matrix products, arithmetic and copies ran while one was open for 2% -> 1% of each run, Pallas kernels for 0% -> 0%
where the time goes in v3:
time: 212 us; the launch traced here: 211 us
  blocking collectives  120 us (57%)
  starting transfers between devices  48.7 us (23%)
  waiting for transfers between devices  28 us (13%)
  Pallas kernels  4.36 us (2%)
  matrix products  4.32 us (2%)
  local copies, waits for them, and re-layouts  2.57 us (1%)
  other arithmetic  2.24 us (1%)
    all_to_all x3, blocking collectives, exchange(): return lax.all_to_all(blocks, 'q', 0, 0)  51.7 us
    all_gather x2, blocking collectives, gradient_of(): grads = lax.all_gather(grads, 'far', axis=0, tiled=True)  31.1 us
    all_to_all x1, blocking collectives, local(): received = lax.all_to_all(sent, MP, 0, 0)  28.7 us
    ppermute x2, starting transfers between devices, local(): theirs = lax.ppermute(given, 'c', swap)  17.7 us
    all_to_all x1, waiting for transfers between devices, local(): lax.all_to_all(sent.astype(BF16).reshape(parts, CORES * share, width), MP...  13.7 us
    all_to_all x1, waiting for transfers between devices, exchange(): return lax.all_to_all(blocks, 'q', 0, 0)  10.8 us
    all_to_all x1, starting transfers between devices, local(): lax.all_to_all(sent.astype(BF16).reshape(parts, CORES * share, width), MP...  9.76 us
    ppermute x1, starting transfers between devices, local(): lax.ppermute(squares, 'c', swap)  9.44 us
  transfers between devices with their start and end apart: 7, of which 6 were waited for; matrix products, arithmetic and copies ran while one was open for 1% of the time, Pallas kernels for 0%

profile of v3, /device:TPU:1, one launch (start us, length us, event | category | flops | bytes accessed | tf_op | source)
XLA Modules:
  0.0 210.7 jit_solution(838684243690627967)
XLA Ops:
  1.4 8.8 %collective-permute-start = (bf16[12,256]{1,0:T(8,128)(2,1)S(1)}, bf16[12,256]{1,0:T(8,128)(2,1)S(1)}, u32[]{:S(2)}, u32[]{:S(2)}) collective-permute-start(bf16[12,256]{1,0:T(8,128)(2,1)S(1)} %dynamic-slice_convert_fusion), channel_id=1, source_target_pairs={{0,8},{8,0},{1,9},{9,1},{2,10},{10,2},{3,11},{11,3},{4,12},{12,4},... | collective-permute-start | bytes 18440 | tf_op jit(solution)/shard_map/ppermute | solution.py:160
  12.5 2.2 %collective-permute-start.1 = (bf16[768,768]{1,0:T(8,128)(2,1)}, bf16[768,768]{1,0:T(8,128)(2,1)S(1)}, u32[]{:S(2)}, u32[]{:S(2)}) collective-permute-start(bf16[768,768]{1,0:T(8,128)(2,1)} %param.5), channel_id=1, source_target_pairs={{0,8},{8,0},{1,9},{9,1},{2,10},{10,2},{3,11},{11,3},{4,12},{12,4},... | collective-permute-start | bytes 3538952 | tf_op jit(solution)/shard_map/ppermute | solution.py:165
  14.7 4.6 %all-to-all-start = ((bf16[32,24,256]{2,1,0:T(8,128)(2,1)}), bf16[32,24,256]{2,1,0:T(8,128)(2,1)}, u32[]{:S(2)}, u32[]{:S(2)}) async-start(bf16[32,24,256]{2,1,0:T(8,128)(2,1)} %spread.1), calls=%async_computation | async-start | bytes 786432 | tf_op jit(solution)/shard_map/all_to_all | solution.py:175
  19.4 1.4 pad_maximum_fusion
  20.8 10.8 %all-to-all-done = bf16[32,24,256]{2,1,0:T(8,128)(2,1)} async-done(((bf16[32,24,256]{2,1,0:T(8,128)(2,1)}), bf16[32,24,256]{2,1,0:T(8,128)(2,1)}, u32[]{:S(2)}, u32[]{:S(2)}) %all-to-all-start) | async-done | bytes 393248 | tf_op jit(solution)/shard_map/all_to_all | solution.py:175
  31.6 2.7 %convolution_convert_fusion = bf16[1536,256]{1,0:T(8,128)(2,1)} fusion(bf16[1536,768]{1,0:T(8,128)(2,1)S(1)} %bitcast.16, bf16[768,256]{1,0:T(8,128)(2,1)} %bitcast.4), kind=kOutput, calls=%fused_computation | convolution fusion | flops 604372992 | bytes 3538944 | tf_op jit(solution)/shard_map/dot_general | solution.py:184
  34.3 9.8 %all-to-all-start.1 = ((bf16[8,192,256]{2,1,0:T(8,128)(2,1)}), bf16[8,192,256]{2,1,0:T(8,128)(2,1)S(1)}, u32[]{:S(2)}, u32[]{:S(2)}) async-start(bf16[8,192,256]{2,1,0:T(8,128)(2,1)} %bitcast.23), calls=%async_computation.1 | async-start | bytes 1572864 | tf_op jit(solution)/shard_map/all_to_all | solution.py:185
  44.0 1.1 fusion
  45.1 5.0 %collective-permute-start.2 = (bf16[96,256]{1,0:T(8,128)(2,1)S(1)}, bf16[96,256]{1,0:T(8,128)(2,1)S(1)}, u32[]{:S(2)}, u32[]{:S(2)}) collective-permute-start(bf16[96,256]{1,0:T(8,128)(2,1)S(1)} %get-tuple-element.16), channel_id=1, source_target_pairs={{0,8},{8,0},{1,9},{9,1},{2,10},{10,2},{3,11},{11,3},{4,12},{12,4},... | collective-permute-start | bytes 147464 | tf_op jit(solution)/shard_map/ppermute | solution.py:172
  50.1 0.9 collective-permute-done.2
  51.0 13.7 %all-to-all-done.1.partial_ref = bf16[8,192,256]{2,1,0:T(8,128)(2,1)S(1)} async-done(((bf16[8,192,256]{2,1,0:T(8,128)(2,1)}), bf16[8,192,256]{2,1,0:T(8,128)(2,1)S(1)}, u32[]{:S(2)}, u32[]{:S(2)}) %all-to-all-start.1) | async-done | bytes 786464 | tf_op jit(solution)/shard_map/all_to_all | solution.py:185
  65.0 4.1 %all_gather.12 = bf16[384,256]{1,0:T(8,128)(2,1)S(1)} all-gather(bf16[192,256]{1,0:T(8,128)(2,1)S(1)} %get-tuple-element.11), channel_id=1, replica_groups=mesh['q'=32,'c'=2,'far'=4,'near'=2] {'near'}, dimensions={0}, use_global_device_ids=true | all-gather | bytes 294912 | tf_op jit(solution)/shard_map/all_gather | solution.py:178
  69.1 15.6 %all_gather.13 = bf16[1536,256]{1,0:T(8,128)(2,1)S(1)} all-gather(bf16[384,256]{1,0:T(8,128)(2,1)S(1)} %all_gather.12), channel_id=1, replica_groups=mesh['q'=32,'c'=2,'far'=4,'near'=2] {'far'}, dimensions={0}, use_global_device_ids=true | all-gather | bytes 983040 | tf_op jit(solution)/shard_map/all_gather | solution.py:179
  84.8 0.8 convolution_convert_fusion.2
  85.6 21.4 %all_to_all.30.received_ref = bf16[32,24,256]{2,1,0:T(8,128)(2,1)S(1)} all-to-all(bf16[32,24,256]{2,1,0:T(8,128)(2,1)S(1)} %bitcast.25), channel_id=1, replica_groups=mesh['q'=32,'c'=2,'far'=4,'near'=2] {'q'}, dimensions={0} | all-to-all | bytes 786432 | tf_op jit(solution)/shard_map/all_to_all | solution.py:175
  107.1 15.3 %all_to_all.31 = bf16[32,24,256]{2,1,0:T(8,128)(2,1)S(1)} all-to-all(bf16[32,24,256]{2,1,0:T(8,128)(2,1)S(1)} %pack.1), channel_id=1, replica_groups=mesh['q'=32,'c'=2,'far'=4,'near'=2] {'q'}, dimensions={0} | all-to-all | bytes 786432 | tf_op jit(solution)/shard_map/all_to_all | solution.py:175
  123.2 9.4 %collective-permute-start.3 = (f32[1,1]{1,0:T(1,128)}, f32[1,1]{1,0:T(1,128)}, u32[]{:S(2)}, u32[]{:S(2)}) collective-permute-start(f32[1,1]{1,0:T(1,128)} %bitcast.8.squares_ref), channel_id=1, source_target_pairs={{0,8},{8,0},{1,9},{9,1},{2,10},{10,2},{3,11},{11,3},{4,12},{12,4},... | collective-permute-start | bytes 20 | tf_op jit(solution)/shard_map/ppermute | solution.py:200
  132.6 1.1 collective-permute-done.3.other_ref
  133.7 2.0 change.1
  135.7 28.7 %all_to_all.32.partial_ref = bf16[8,200,256]{2,1,0:T(8,128)(2,1)S(1)} all-to-all(bf16[8,200,256]{2,1,0:T(8,128)(2,1)S(1)} %change.1), channel_id=1, replica_groups=mesh['q'=32,'c'=2,'far'=4,'near'=2] {'far','near'}, dimensions={0} | all-to-all | bytes 1638400 | tf_op jit(solution)/shard_map/all_to_all | solution.py:203
  164.8 4.1 %all_gather.14 = bf16[384,256]{1,0:T(8,128)(2,1)S(1)} all-gather(bf16[192,256]{1,0:T(8,128)(2,1)S(1)} %second_heads.1), channel_id=1, replica_groups=mesh['q'=32,'c'=2,'far'=4,'near'=2] {'near'}, dimensions={0}, use_global_device_ids=true | all-gather | bytes 294912 | tf_op jit(solution)/shard_map/all_gather | solution.py:178
  168.9 15.4 %all_gather.15 = bf16[1536,256]{1,0:T(8,128)(2,1)S(1)} all-gather(bf16[384,256]{1,0:T(8,128)(2,1)S(1)} %all_gather.14), channel_id=1, replica_groups=mesh['q'=32,'c'=2,'far'=4,'near'=2] {'far'}, dimensions={0}, use_global_device_ids=true | all-gather | bytes 983040 | tf_op jit(solution)/shard_map/all_gather | solution.py:179
  185.2 15.0 %all_to_all.33.received_ref = bf16[32,24,256]{2,1,0:T(8,128)(2,1)S(1)} all-to-all(bf16[32,24,256]{2,1,0:T(8,128)(2,1)S(1)} %bitcast.24), channel_id=1, replica_groups=mesh['q'=32,'c'=2,'far'=4,'near'=2] {'q'}, dimensions={0} | all-to-all | bytes 786432 | tf_op jit(solution)/shard_map/all_to_all | solution.py:175
  200.3 8.9 %collective-permute-start.4 = (f32[12,256]{1,0:T(8,128)S(1)}, f32[12,256]{1,0:T(8,128)S(1)}, u32[]{:S(2)}, u32[]{:S(2)}) collective-permute-start(f32[12,256]{1,0:T(8,128)S(1)} %get-tuple-element.14), channel_id=1, source_target_pairs={{0,8},{8,0},{1,9},{9,1},{2,10},{10,2},{3,11},{11,3},{4,12},{12,4},... | collective-permute-start | bytes 36872 | tf_op jit(solution)/shard_map/ppermute | solution.py:208
  (21 shorter events, 7.1 us)
Async XLA Ops:
  1.4 9.6 %collective-permute-start = (bf16[12,256]{1,0:T(8,128)(2,1)S(1)}, bf16[12,256]{1,0:T(8,128)(2,1)S(1)}, u32[]{:S(2)}, u32[]{:S(2)}) collective-permute-start(bf16[12,256]{1,0:T(8,128)(2,1)S(1)} %dynamic-slice_convert_fusion), channel_id=1, source_target_pairs={{0,8},{8,0},{1,9},{9,1},{2,10},{10,2},{3,11},{11,3},{4,12},{12,4},... | collective-permute-start | bytes 18440 | tf_op jit(solution)/shard_map/ppermute | solution.py:160
  11.0 0.8 copy-start
  12.5 6.9 %collective-permute-start.1 = (bf16[768,768]{1,0:T(8,128)(2,1)}, bf16[768,768]{1,0:T(8,128)(2,1)S(1)}, u32[]{:S(2)}, u32[]{:S(2)}) collective-permute-start(bf16[768,768]{1,0:T(8,128)(2,1)} %param.5), channel_id=1, source_target_pairs={{0,8},{8,0},{1,9},{9,1},{2,10},{10,2},{3,11},{11,3},{4,12},{12,4},... | collective-permute-start | bytes 3538952 | tf_op jit(solution)/shard_map/ppermute | solution.py:165
  14.7 16.9 %all-to-all-start = ((bf16[32,24,256]{2,1,0:T(8,128)(2,1)}), bf16[32,24,256]{2,1,0:T(8,128)(2,1)}, u32[]{:S(2)}, u32[]{:S(2)}) async-start(bf16[32,24,256]{2,1,0:T(8,128)(2,1)} %spread.1), calls=%async_computation | async-start | bytes 786432 | tf_op jit(solution)/shard_map/all_to_all | solution.py:175
  34.3 30.3 %all-to-all-start.1 = ((bf16[8,192,256]{2,1,0:T(8,128)(2,1)}), bf16[8,192,256]{2,1,0:T(8,128)(2,1)S(1)}, u32[]{:S(2)}, u32[]{:S(2)}) async-start(bf16[8,192,256]{2,1,0:T(8,128)(2,1)} %bitcast.23), calls=%async_computation.1 | async-start | bytes 1572864 | tf_op jit(solution)/shard_map/all_to_all | solution.py:185
  45.1 5.8 %collective-permute-start.2 = (bf16[96,256]{1,0:T(8,128)(2,1)S(1)}, bf16[96,256]{1,0:T(8,128)(2,1)S(1)}, u32[]{:S(2)}, u32[]{:S(2)}) collective-permute-start(bf16[96,256]{1,0:T(8,128)(2,1)S(1)} %get-tuple-element.16), channel_id=1, source_target_pairs={{0,8},{8,0},{1,9},{9,1},{2,10},{10,2},{3,11},{11,3},{4,12},{12,4},... | collective-permute-start | bytes 147464 | tf_op jit(solution)/shard_map/ppermute | solution.py:172
  123.2 10.5 %collective-permute-start.3 = (f32[1,1]{1,0:T(1,128)}, f32[1,1]{1,0:T(1,128)}, u32[]{:S(2)}, u32[]{:S(2)}) collective-permute-start(f32[1,1]{1,0:T(1,128)} %bitcast.8.squares_ref), channel_id=1, source_target_pairs={{0,8},{8,0},{1,9},{9,1},{2,10},{10,2},{3,11},{11,3},{4,12},{12,4},... | collective-permute-start | bytes 20 | tf_op jit(solution)/shard_map/ppermute | solution.py:200
  184.4 25.7 %copy-start.1 = (f32[12,512]{1,0:T(8,128)S(1)}, f32[12,512]{1,0:T(8,128)}, u32[]{:S(2)}) copy-start(f32[12,512]{1,0:T(8,128)} %weights_ref.3) | copy-start | bytes 73732
  184.4 25.7 %copy-start.2 = (f32[12,512]{1,0:T(8,128)S(1)}, f32[12,512]{1,0:T(8,128)}, u32[]{:S(2)}) copy-start(f32[12,512]{1,0:T(8,128)} %one_ref.1) | copy-start | bytes 73732
  184.4 25.7 %copy-start.3 = (f32[12,512]{1,0:T(8,128)S(1)}, f32[12,512]{1,0:T(8,128)}, u32[]{:S(2)}) copy-start(f32[12,512]{1,0:T(8,128)} %two_ref.1) | copy-start | bytes 73732
  200.3 9.8 %collective-permute-start.4 = (f32[12,256]{1,0:T(8,128)S(1)}, f32[12,256]{1,0:T(8,128)S(1)}, u32[]{:S(2)}, u32[]{:S(2)}) collective-permute-start(f32[12,256]{1,0:T(8,128)S(1)} %get-tuple-element.14), channel_id=1, source_target_pairs={{0,8},{8,0},{1,9},{9,1},{2,10},{10,2},{3,11},{11,3},{4,12},{12,4},... | collective-permute-start | bytes 36872 | tf_op jit(solution)/shard_map/ppermute | solution.py:208

commit v4 on v3

--- a/solution.py
+++ b/solution.py
@@ -35,12 +35,6 @@
     lanes = lax.broadcasted_iota(jnp.int32, shape, len(shape) - 1)
     picked = jnp.where(lanes == 0, high, jnp.where(lanes == 1, middle, jnp.where(lanes == 2, low, 0.0)))
     return jnp.where(rows == row, picked, 0.0)
-
-
-def scalar_in(block, row):
-    rows = lax.broadcasted_iota(jnp.int32, block.shape, len(block.shape) - 2)
-    lanes = lax.broadcasted_iota(jnp.int32, block.shape, len(block.shape) - 1)
-    return jnp.sum(jnp.where((rows == row) & (lanes < 3), block.astype(F32), 0.0))
 
 
 def call(kernel, name, out_shape, *operands, cost=(0, 0)):
@@ -58,13 +52,13 @@
 
 
 def head_kernel(second, partial_ref, *refs):
-    base_ref = refs[0] if second else None
-    cotangent_ref = refs[1] if second else refs[0]
+    squares_ref, base_ref = refs[:2] if second else (None, None)
+    cotangent_ref = refs[2] if second else refs[0]
     out_ref = refs[-1]
     tokens, width = cotangent_ref.shape
     if second:
-        squares = scalar_in(partial_ref[:, tokens : tokens + TAIL, 0:HEAD_DIM], 0)
-        scale = radius * lax.rsqrt(jnp.full((1, HEAD_DIM), squares + 1e-06, F32))
+        squares = squares_ref[0:1, :] + squares_ref[TAIL : TAIL + 1, :]
+        scale = radius * lax.rsqrt(squares + 1e-06)
     for head in range(width // HEAD_DIM):
         lanes = slice(head * HEAD_DIM, (head + 1) * HEAD_DIM)
         queries = partial_ref[0, 0:tokens, lanes].astype(F32)
@@ -88,10 +82,11 @@
     return jnp.where(core == 0, one, two), jnp.where(core == 0, two, one)
 
 
-def spread_kernel(core_ref, weights_ref, theirs_ref, out_ref):
-    width = theirs_ref.shape[1]
-    mine = swapped(core_ref[0, 0], weights_ref[:, :width], weights_ref[:, width:])[0]
-    pair = swapped(core_ref[0, 0], mine, theirs_ref[...].astype(F32))
+def spread_kernel(core_ref, weights_ref, out_ref):
+    width = out_ref.shape[2]
+    pair = []
+    for side in range(CORES):
+        pair.append(swapped(core_ref[0, 0], weights_ref[side, :, :width], weights_ref[side, :, width:])[0])
     block = jnp.concatenate(pair, axis=0).astype(BF16)
     for part in range(out_ref.shape[0]):
         out_ref[part] = block
@@ -106,21 +101,26 @@
         out_ref[part] = block
 
 
-def fold_kernel(loss_scale, core_ref, received_ref, kept_ref, given_ref):
+def fold_kernel(loss_scale, received_ref, out_ref):
     total = received_ref[0].astype(F32)
     for part in range(1, received_ref.shape[0]):
         total = total + received_ref[part].astype(F32)
-    total = total * loss_scale
-    rows = kept_ref.shape[0]
-    kept_ref[...], given_ref[...] = swapped(core_ref[0, 0], total[:rows], total[rows:])
-
-
-def update_kernel(core_ref, mine_ref, theirs_ref, weights_ref, one_ref, two_ref, *out_refs):
-    width = mine_ref.shape[1]
+    out_ref[...] = total * loss_scale
+
+
+def update_kernel(core_ref, second_ref, weights_ref, one_ref, two_ref, *out_refs):
+    rows = weights_ref.shape[0]
+    width = second_ref.shape[1]
     correct_one = 1.0 - decay_one**step_count
     correct_two = 1.0 - decay_two**step_count
-    for side, second in enumerate(swapped(core_ref[0, 0], mine_ref[...], theirs_ref[...])):
+    for side in range(CORES):
+        start = side * CORES * rows
         lanes = slice(side * width, (side + 1) * width)
+        second = swapped(
+            core_ref[0, 0],
+            second_ref[start : start + rows, :],
+            second_ref[start + rows : start + CORES * rows, :],
+        )[0]
         weights = weights_ref[:, lanes]
         new_one = decay_one * one_ref[:, lanes] + (1.0 - decay_one) * second
         new_two = decay_two * two_ref[:, lanes] + (1.0 - decay_two) * second * second
@@ -130,17 +130,28 @@
         out_refs[2][:, lanes] = new_two
 
 
-def change_kernel(tokens_ref, first_ref, squares_ref, other_ref, out_ref):
+def total_kernel(received_ref, out_ref):
+    parts, share, _ = received_ref.shape
+    block = received_ref[0, share - TAIL : share, 0:HEAD_DIM].astype(F32)
+    for part in range(1, parts):
+        block = block + received_ref[part, share - TAIL : share, 0:HEAD_DIM].astype(F32)
+    out_ref[...] = jnp.full(out_ref.shape, jnp.sum(block), F32)
+
+
+def queries_kernel(second, tokens_ref, first_ref, out_ref):
     parts, share, width = out_ref.shape
-    share = share - TAIL
-    tail = pieces_of(squares_ref[...] + other_ref[...], (TAIL, width), 0).astype(BF16)
+    if second:
+        share = share - TAIL
+        first = first_ref[...].astype(F32)
+        tail = pieces_of(jnp.sum(first * first), (TAIL, width), 0).astype(BF16)
     step = 2
     for group in range(parts // step):
         picked = slice(group * step * share, (group + 1) * step * share)
         value = jnp.dot(tokens_ref[picked, :], first_ref[...], preferred_element_type=F32)
         for part in range(step):
             out_ref[group * step + part, 0:share, :] = value[part * share : (part + 1) * share].astype(BF16)
-            out_ref[group * step + part, share : share + TAIL, :] = tail
+            if second:
+                out_ref[group * step + part, share : share + TAIL, :] = tail
 
 
 def local(tokens, cotangent, weights, moment_one, moment_two):
@@ -156,10 +167,8 @@
     swap = [(0, 1), (1, 0)]
 
     which = core.reshape(1, 1).astype(jnp.int32)
-    given = lax.dynamic_slice_in_dim(weights, (1 - core) * width, width, 1).astype(BF16)
-    theirs = lax.ppermute(given, "c", swap)
     blocks = shape((groups, CORES * rows, width), BF16)
-    spread = call(spread_kernel, "spread", blocks, which, weights, theirs)
+    spread = call(spread_kernel, "spread", blocks, which, lax.all_gather(weights, "c", axis=0))
     spread, tokens = lax.optimization_barrier((spread, tokens))
 
     theirs = lax.ppermute(tokens, "c", swap)
@@ -173,6 +182,16 @@
 
     def exchange(blocks):
         return lax.all_to_all(blocks, "q", 0, 0)
+
+    def queries_of(second, blocks):
+        return call(
+            functools.partial(queries_kernel, second),
+            "second_queries" if second else "first_queries",
+            shape((parts, CORES * share + TAIL * second, width), BF16),
+            tokens,
+            exchange(blocks).reshape(depth, width),
+            cost=(2 * CORES * count * depth * width, 2 * CORES * count * depth),
+        )
 
     def gradient_of(grads):
         grads = lax.all_gather(grads, "near", axis=0, tiled=True)
@@ -180,36 +199,29 @@
         summed = lax.dot_general(tokens, grads, (((0,), (0,)), ((), ())), preferred_element_type=F32)
         return exchange(summed.astype(BF16).reshape(groups, CORES * rows, width))
 
-    gathered = exchange(spread)
-    sent = jnp.dot(tokens, gathered.reshape(depth, width), preferred_element_type=F32)
-    received = lax.all_to_all(sent.astype(BF16).reshape(parts, CORES * share, width), MP, 0, 0)
+    sent = queries_of(False, spread)
+    received = lax.all_to_all(sent, MP, 0, 0)
     outs = (shape((CORES * share, width), F32), shape((CORES * share, width), BF16))
     queries, grads = call(functools.partial(head_kernel, False), "first_heads", outs, received, cot)
     received = gradient_of(grads)
 
     packed = call(functools.partial(pack_kernel, loss_scale), "pack", blocks, received)
-    first = exchange(packed).reshape(depth, width)
-    squares = jnp.sum(jnp.square(first.astype(F32))).reshape(1, 1)
-    sent = call(
-        change_kernel,
-        "change",
-        shape((parts, CORES * share + TAIL, width), BF16),
-        tokens,
-        first,
-        squares,
-        lax.ppermute(squares, "c", swap),
-        cost=(2 * CORES * count * depth * width, 2 * CORES * count * depth),
+    sent = queries_of(True, packed)
+    received = lax.all_to_all(sent, MP, 0, 0)
+    squares = call(total_kernel, "total", shape((TAIL, HEAD_DIM), F32), received)
+    squares = lax.all_gather(squares, "c", axis=0, tiled=True)
+    grads = call(
+        functools.partial(head_kernel, True), "second_heads", outs[1], received, squares, queries, cot
     )
-    received = lax.all_to_all(sent, MP, 0, 0)
-    grads = call(functools.partial(head_kernel, True), "second_heads", outs[1], received, queries, cot)
-    half = shape((rows, width), F32)
-    received = gradient_of(grads)
-    mine, given = call(functools.partial(fold_kernel, loss_scale), "fold", (half, half), which, received)
-    theirs = lax.ppermute(given, "c", swap)
+    second = call(
+        functools.partial(fold_kernel, loss_scale),
+        "fold",
+        shape((CORES * rows, width), F32),
+        gradient_of(grads),
+    )
+    second = lax.all_gather(second, "c", axis=0, tiled=True)
     whole = shape((rows, columns), F32)
-    return call(
-        update_kernel, "update", (whole,) * 3, which, mine, theirs, weights, moment_one, moment_two
-    )
+    return call(update_kernel, "update", (whole,) * 3, which, second, weights, moment_one, moment_two)
 
 
 def solution(mesh):

time: 212 us -> 202 us (0.953)
  starting transfers between devices: 48.7 us -> 21.6 us
  blocking collectives: 120 us -> 145 us
  waiting for transfers between devices: 28 us -> 23.9 us
  matrix products: 4.32 us -> 1.64 us
    ppermute x3 -> x0, starting transfers between devices: 27.2 us -> none  [the longest x2 17.7 us: local(): theirs = lax.ppermute(given, 'c', swap)]
    all_gather x0 -> x3, blocking collectives: none -> 25.6 us  [the longest x1 8.78 us: local(): second = lax.all_gather(second, 'c', axis=0, tiled=True)]
    all_to_all x1, blocking collectives: 28.7 us -> 25.7 us  [local(): received = lax.all_to_all(sent, MP, 0, 0)]
    ppermute x3 -> x0, waiting for transfers between devices: 2.69 us -> none  [the longest x2 1.62 us: local(): theirs = lax.ppermute(given, 'c', swap)]
    dot_general x1 -> x0, matrix products: 2.68 us -> none  [local(): jnp.dot(tokens, gathered.reshape(depth, width), preferred_element_type=F32)]
    all_to_all x3, blocking collectives: 51.7 us -> 54.1 us  [exchange(): return lax.all_to_all(blocks, 'q', 0, 0)]
    pallas_call x7 -> x9, Pallas kernels: 4.36 us -> 4.94 us  [call(): pl.pallas_call(kernel, in_specs=[smem if operand.dtype == jnp.int32 else...]
  transfers between devices with their start and end apart: 7 -> 4, of which waited for: 6 -> 3; matrix products, arithmetic and copies ran while one was open for 1% -> 1% of each run, Pallas kernels for 0% -> 0%
where the time goes in v4:
time: 202 us; the launch traced here: 201 us
  blocking collectives  145 us (72%)
  waiting for transfers between devices  23.9 us (12%)
  starting transfers between devices  21.6 us (11%)
  Pallas kernels  4.94 us (2%)
  local copies, waits for them, and re-layouts  2.1 us (1%)
    all_to_all x3, blocking collectives, exchange(): return lax.all_to_all(blocks, 'q', 0, 0)  54.1 us
    all_gather x2, blocking collectives, gradient_of(): grads = lax.all_gather(grads, 'far', axis=0, tiled=True)  30.4 us
    all_to_all x1, blocking collectives, local(): received = lax.all_to_all(sent, MP, 0, 0)  25.7 us
    all_to_all x1, waiting for transfers between devices, local(): received = lax.all_to_all(sent, MP, 0, 0)  13.7 us
    all_to_all x1, starting transfers between devices, local(): received = lax.all_to_all(sent, MP, 0, 0)  10 us
    all_to_all x1, waiting for transfers between devices, exchange(): return lax.all_to_all(blocks, 'q', 0, 0)  9.35 us
    all_gather x2, blocking collectives, gradient_of(): grads = lax.all_gather(grads, 'near', axis=0, tiled=True)  8.9 us
    all_gather x1, blocking collectives, local(): second = lax.all_gather(second, 'c', axis=0, tiled=True)  8.78 us
  transfers between devices with their start and end apart: 4, of which 3 were waited for; matrix products, arithmetic and copies ran while one was open for 1% of the time, Pallas kernels for 0%

profile of v4, /device:TPU:1, one launch (start us, length us, event | category | flops | bytes accessed | tf_op | source)
XLA Modules:
  0.0 201.3 jit_solution(1854034320199225763)
XLA Ops:
  0.6 8.6 %all-gather.1.weights_ref = f32[2,12,512]{2,1,0:T(8,128)S(1)} all-gather(f32[1,12,512]{2,1,0:T(8,128)} %bitcast.19), channel_id=2, replica_groups=mesh['q'=32,'c'=2,'far'=4,'near'=2] {'c'}, dimensions={0}, use_global_device_ids=true | all-gather | bytes 73728 | tf_op jit(solution)/shard_map/all_gather | solution.py:171
  10.0 2.2 %collective-permute-start = (bf16[768,768]{1,0:T(8,128)(2,1)}, bf16[768,768]{1,0:T(8,128)(2,1)S(1)}, u32[]{:S(2)}, u32[]{:S(2)}) collective-permute-start(bf16[768,768]{1,0:T(8,128)(2,1)} %param.5), channel_id=1, source_target_pairs={{0,8},{8,0},{1,9},{9,1},{2,10},{10,2},{3,11},{11,3},{4,12},{12,4},... | collective-permute-start | bytes 3538952 | tf_op jit(solution)/shard_map/ppermute | solution.py:174
  12.3 4.3 %all-to-all-start = ((bf16[32,24,256]{2,1,0:T(8,128)(2,1)}), bf16[32,24,256]{2,1,0:T(8,128)(2,1)S(1)}, u32[]{:S(2)}, u32[]{:S(2)}) async-start(bf16[32,24,256]{2,1,0:T(8,128)(2,1)} %spread.1), calls=%async_computation | async-start | bytes 786432 | tf_op jit(solution)/shard_map/all_to_all | solution.py:184
  16.6 1.0 copy-done.3
  17.6 1.8 pad_maximum_fusion
  19.4 9.3 %all-to-all-done = bf16[32,24,256]{2,1,0:T(8,128)(2,1)S(1)} async-done(((bf16[32,24,256]{2,1,0:T(8,128)(2,1)}), bf16[32,24,256]{2,1,0:T(8,128)(2,1)S(1)}, u32[]{:S(2)}, u32[]{:S(2)}) %all-to-all-start) | async-done | bytes 393248 | tf_op jit(solution)/shard_map/all_to_all | solution.py:184
  28.8 1.7 first_queries.1
  30.4 10.0 %all-to-all-start.1 = ((bf16[8,192,256]{2,1,0:T(8,128)(2,1)}), bf16[8,192,256]{2,1,0:T(8,128)(2,1)S(1)}, u32[]{:S(2)}, u32[]{:S(2)}) async-start(bf16[8,192,256]{2,1,0:T(8,128)(2,1)} %first_queries.1), calls=%async_computation.1 | async-start | bytes 1572864 | tf_op jit(solution)/shard_map/all_to_all | solution.py:203
  40.5 1.1 fusion
  41.5 5.0 %collective-permute-start.1 = (bf16[96,256]{1,0:T(8,128)(2,1)S(1)}, bf16[96,256]{1,0:T(8,128)(2,1)S(1)}, u32[]{:S(2)}, u32[]{:S(2)}) collective-permute-start(bf16[96,256]{1,0:T(8,128)(2,1)S(1)} %get-tuple-element.12), channel_id=1, source_target_pairs={{0,8},{8,0},{1,9},{9,1},{2,10},{10,2},{3,11},{11,3},{4,12},{12,4},... | collective-permute-start | bytes 147464 | tf_op jit(solution)/shard_map/ppermute | solution.py:181
  46.5 0.9 collective-permute-done.1
  47.4 13.7 %all-to-all-done.1.partial_ref = bf16[8,192,256]{2,1,0:T(8,128)(2,1)S(1)} async-done(((bf16[8,192,256]{2,1,0:T(8,128)(2,1)}), bf16[8,192,256]{2,1,0:T(8,128)(2,1)S(1)}, u32[]{:S(2)}, u32[]{:S(2)}) %all-to-all-start.1) | async-done | bytes 786464 | tf_op jit(solution)/shard_map/all_to_all | solution.py:203
  61.4 4.1 %all_gather.26 = bf16[384,256]{1,0:T(8,128)(2,1)S(1)} all-gather(bf16[192,256]{1,0:T(8,128)(2,1)S(1)} %get-tuple-element.9), channel_id=1, replica_groups=mesh['q'=32,'c'=2,'far'=4,'near'=2] {'near'}, dimensions={0}, use_global_device_ids=true | all-gather | bytes 294912 | tf_op jit(solution)/shard_map/all_gather | solution.py:197
  65.6 15.6 %all_gather.27 = bf16[1536,256]{1,0:T(8,128)(2,1)S(1)} all-gather(bf16[384,256]{1,0:T(8,128)(2,1)S(1)} %all_gather.26), channel_id=1, replica_groups=mesh['q'=32,'c'=2,'far'=4,'near'=2] {'far'}, dimensions={0}, use_global_device_ids=true | all-gather | bytes 983040 | tf_op jit(solution)/shard_map/all_gather | solution.py:198
  81.2 0.8 convolution_convert_fusion.1
  82.0 21.4 %all_to_all.30.received_ref = bf16[32,24,256]{2,1,0:T(8,128)(2,1)S(1)} all-to-all(bf16[32,24,256]{2,1,0:T(8,128)(2,1)S(1)} %bitcast.23), channel_id=1, replica_groups=mesh['q'=32,'c'=2,'far'=4,'near'=2] {'q'}, dimensions={0} | all-to-all | bytes 786432 | tf_op jit(solution)/shard_map/all_to_all | solution.py:184
  103.5 15.4 %all_to_all.31 = bf16[32,24,256]{2,1,0:T(8,128)(2,1)S(1)} all-to-all(bf16[32,24,256]{2,1,0:T(8,128)(2,1)S(1)} %pack.1), channel_id=1, replica_groups=mesh['q'=32,'c'=2,'far'=4,'near'=2] {'q'}, dimensions={0} | all-to-all | bytes 786432 | tf_op jit(solution)/shard_map/all_to_all | solution.py:184
  119.7 25.7 %all_to_all.32.received_ref.partial_ref = bf16[8,200,256]{2,1,0:T(8,128)(2,1)S(1)} all-to-all(bf16[8,200,256]{2,1,0:T(8,128)(2,1)S(1)} %second_queries.1), channel_id=1, replica_groups=mesh['q'=32,'c'=2,'far'=4,'near'=2] {'far','near'}, dimensions={0} | all-to-all | bytes 1638400 | tf_op jit(solution)/shard_map/all_to_all | solution.py:210
  145.5 8.3 %all_gather.28.refs_0_ = f32[16,128]{1,0:T(8,128)S(1)} all-gather(f32[8,128]{1,0:T(8,128)S(1)} %total.1), channel_id=1, replica_groups=mesh['q'=32,'c'=2,'far'=4,'near'=2] {'c'}, dimensions={0}, use_global_device_ids=true | all-gather | bytes 12288 | tf_op jit(solution)/shard_map/all_gather | solution.py:212
  154.2 4.8 %all_gather.29 = bf16[384,256]{1,0:T(8,128)(2,1)S(1)} all-gather(bf16[192,256]{1,0:T(8,128)(2,1)S(1)} %second_heads.1), channel_id=1, replica_groups=mesh['q'=32,'c'=2,'far'=4,'near'=2] {'near'}, dimensions={0}, use_global_device_ids=true | all-gather | bytes 294912 | tf_op jit(solution)/shard_map/all_gather | solution.py:197
  158.9 14.7 %all_gather.30 = bf16[1536,256]{1,0:T(8,128)(2,1)S(1)} all-gather(bf16[384,256]{1,0:T(8,128)(2,1)S(1)} %all_gather.29), channel_id=1, replica_groups=mesh['q'=32,'c'=2,'far'=4,'near'=2] {'far'}, dimensions={0}, use_global_device_ids=true | all-gather | bytes 983040 | tf_op jit(solution)/shard_map/all_gather | solution.py:198
  173.7 0.8 convolution_convert_fusion
  174.5 17.3 %all_to_all.33.received_ref = bf16[32,24,256]{2,1,0:T(8,128)(2,1)S(1)} all-to-all(bf16[32,24,256]{2,1,0:T(8,128)(2,1)S(1)} %bitcast.22), channel_id=1, replica_groups=mesh['q'=32,'c'=2,'far'=4,'near'=2] {'q'}, dimensions={0} | all-to-all | bytes 786432 | tf_op jit(solution)/shard_map/all_to_all | solution.py:184
  191.9 8.8 %all_gather.31.second_ref = f32[48,256]{1,0:T(8,128)S(1)} all-gather(f32[24,256]{1,0:T(8,128)S(1)} %fold.1), channel_id=1, replica_groups=mesh['q'=32,'c'=2,'far'=4,'near'=2] {'c'}, dimensions={0}, use_global_device_ids=true | all-gather | bytes 73728 | tf_op jit(solution)/shard_map/all_gather | solution.py:222
  (17 shorter events, 3.3 us)
Async XLA Ops:
  10.0 6.6 %collective-permute-start = (bf16[768,768]{1,0:T(8,128)(2,1)}, bf16[768,768]{1,0:T(8,128)(2,1)S(1)}, u32[]{:S(2)}, u32[]{:S(2)}) collective-permute-start(bf16[768,768]{1,0:T(8,128)(2,1)} %param.5), channel_id=1, source_target_pairs={{0,8},{8,0},{1,9},{9,1},{2,10},{10,2},{3,11},{11,3},{4,12},{12,4},... | collective-permute-start | bytes 3538952 | tf_op jit(solution)/shard_map/ppermute | solution.py:174
  12.3 16.5 %all-to-all-start = ((bf16[32,24,256]{2,1,0:T(8,128)(2,1)}), bf16[32,24,256]{2,1,0:T(8,128)(2,1)S(1)}, u32[]{:S(2)}, u32[]{:S(2)}) async-start(bf16[32,24,256]{2,1,0:T(8,128)(2,1)} %spread.1), calls=%async_computation | async-start | bytes 786432 | tf_op jit(solution)/shard_map/all_to_all | solution.py:184
  16.6 1.0 copy-start.3
  30.4 30.6 %all-to-all-start.1 = ((bf16[8,192,256]{2,1,0:T(8,128)(2,1)}), bf16[8,192,256]{2,1,0:T(8,128)(2,1)S(1)}, u32[]{:S(2)}, u32[]{:S(2)}) async-start(bf16[8,192,256]{2,1,0:T(8,128)(2,1)} %first_queries.1), calls=%async_computation.1 | async-start | bytes 1572864 | tf_op jit(solution)/shard_map/all_to_all | solution.py:203
  41.5 5.8 %collective-permute-start.1 = (bf16[96,256]{1,0:T(8,128)(2,1)S(1)}, bf16[96,256]{1,0:T(8,128)(2,1)S(1)}, u32[]{:S(2)}, u32[]{:S(2)}) collective-permute-start(bf16[96,256]{1,0:T(8,128)(2,1)S(1)} %get-tuple-element.12), channel_id=1, source_target_pairs={{0,8},{8,0},{1,9},{9,1},{2,10},{10,2},{3,11},{11,3},{4,12},{12,4},... | collective-permute-start | bytes 147464 | tf_op jit(solution)/shard_map/ppermute | solution.py:181
  173.7 27.0 %copy-start = (f32[12,512]{1,0:T(8,128)S(1)}, f32[12,512]{1,0:T(8,128)}, u32[]{:S(2)}) copy-start(f32[12,512]{1,0:T(8,128)} %weights_ref.1) | copy-start | bytes 73732
  173.7 27.0 %copy-start.1 = (f32[12,512]{1,0:T(8,128)S(1)}, f32[12,512]{1,0:T(8,128)}, u32[]{:S(2)}) copy-start(f32[12,512]{1,0:T(8,128)} %one_ref.1) | copy-start | bytes 73732
  173.7 27.0 %copy-start.2 = (f32[12,512]{1,0:T(8,128)S(1)}, f32[12,512]{1,0:T(8,128)}, u32[]{:S(2)}) copy-start(f32[12,512]{1,0:T(8,128)} %two_ref.1) | copy-start | bytes 73732

commit v5 on v4

--- a/solution.py
+++ b/solution.py
@@ -179,6 +179,7 @@
     kept = lax.dynamic_slice_in_dim(cot, core * width, width, 1)
     given = lax.dynamic_slice_in_dim(cot, (1 - core) * width, width, 1)
     cot = jnp.concatenate([kept, lax.ppermute(given, "c", swap)], axis=0)
+    tokens, cot = lax.optimization_barrier((tokens, cot))
 
     def exchange(blocks):
         return lax.all_to_all(blocks, "q", 0, 0)

time: 202 us -> 193 us (0.955)
  blocking collectives: 145 us -> 167 us
  waiting for transfers between devices: 23.9 us -> 5.95 us
  starting transfers between devices: 21.6 us -> 8.83 us
    all_to_all x1 -> x2, blocking collectives: 25.7 us -> 47.7 us  [local(): received = lax.all_to_all(sent, MP, 0, 0)]
    all_to_all x1 -> x0, waiting for transfers between devices: 13.7 us -> none  [local(): received = lax.all_to_all(sent, MP, 0, 0)]
    all_to_all x1 -> x0, starting transfers between devices: 10 us -> none  [local(): received = lax.all_to_all(sent, MP, 0, 0)]
    all_to_all x1, waiting for transfers between devices: 9.35 us -> 5.08 us  [exchange(): return lax.all_to_all(blocks, 'q', 0, 0)]
    all_gather x1, blocking collectives: 8.26 us -> 11.7 us  [local(): squares = lax.all_gather(squares, 'c', axis=0, tiled=True)]
    ppermute x1, starting transfers between devices: 4.96 us -> 2.27 us  [local(): cot = jnp.concatenate([kept, lax.ppermute(given, 'c', swap)], axis=0)]
    all_to_all x3, blocking collectives: 54.1 us -> 51.6 us  [exchange(): return lax.all_to_all(blocks, 'q', 0, 0)]
  transfers between devices with their start and end apart: 4 -> 3, of which waited for: 3 -> 2; matrix products, arithmetic and copies ran while one was open for 1% -> 1% of each run, Pallas kernels for 0% -> 0%
where the time goes in v5:
time: 193 us
  blocking collectives  167 us (87%)
  starting transfers between devices  8.83 us (5%)
  waiting for transfers between devices  5.95 us (3%)
  Pallas kernels  4.04 us (2%)
  local copies, waits for them, and re-layouts  2.12 us (1%)
    all_to_all x3, blocking collectives, exchange(): return lax.all_to_all(blocks, 'q', 0, 0)  51.6 us
    all_to_all x2, blocking collectives, local(): received = lax.all_to_all(sent, MP, 0, 0)  47.7 us
    all_gather x2, blocking collectives, gradient_of(): grads = lax.all_gather(grads, 'far', axis=0, tiled=True)  30.4 us
    all_gather x1, blocking collectives, local(): squares = lax.all_gather(squares, 'c', axis=0, tiled=True)  11.7 us
    all_gather x2, blocking collectives, gradient_of(): grads = lax.all_gather(grads, 'near', axis=0, tiled=True)  9.13 us
    all_gather x1, blocking collectives, local(): lax.all_gather(weights, 'c', axis=0)  8.6 us
    all_gather x1, blocking collectives, local(): second = lax.all_gather(second, 'c', axis=0, tiled=True)  8.31 us
    all_to_all x1, waiting for transfers between devices, exchange(): return lax.all_to_all(blocks, 'q', 0, 0)  5.08 us
  transfers between devices with their start and end apart: 3, of which 2 were waited for; matrix products, arithmetic and copies ran while one was open for 1% of the time, Pallas kernels for 0%

profile of v5, /device:TPU:1, one launch (start us, length us, event | category | flops | bytes accessed | tf_op | source)
XLA Modules:
  0.0 192.6 jit_solution(289560056996114842)
XLA Ops:
  0.6 8.6 %all-gather.1.weights_ref = f32[2,12,512]{2,1,0:T(8,128)S(1)} all-gather(f32[1,12,512]{2,1,0:T(8,128)} %bitcast.19), channel_id=2, replica_groups=mesh['q'=32,'c'=2,'far'=4,'near'=2] {'c'}, dimensions={0}, use_global_device_ids=true | all-gather | bytes 73728 | tf_op jit(solution)/shard_map/all_gather | solution.py:171
  9.2 0.8 spread.1
  10.0 2.2 %collective-permute-start = (bf16[768,768]{1,0:T(8,128)(2,1)}, bf16[768,768]{1,0:T(8,128)(2,1)S(1)}, u32[]{:S(2)}, u32[]{:S(2)}) collective-permute-start(bf16[768,768]{1,0:T(8,128)(2,1)} %param.5), channel_id=1, source_target_pairs={{0,8},{8,0},{1,9},{9,1},{2,10},{10,2},{3,11},{11,3},{4,12},{12,4},... | collective-permute-start | bytes 3538952 | tf_op jit(solution)/shard_map/ppermute | solution.py:174
  12.3 4.3 %all-to-all-start = ((bf16[32,24,256]{2,1,0:T(8,128)(2,1)}), bf16[32,24,256]{2,1,0:T(8,128)(2,1)S(1)}, u32[]{:S(2)}, u32[]{:S(2)}) async-start(bf16[32,24,256]{2,1,0:T(8,128)(2,1)} %spread.1), calls=%async_computation | async-start | bytes 786432 | tf_op jit(solution)/shard_map/all_to_all | solution.py:185
  16.6 1.1 fusion
  17.7 2.3 %collective-permute-start.1 = (bf16[96,256]{1,0:T(8,128)(2,1)S(1)}, bf16[96,256]{1,0:T(8,128)(2,1)S(1)}, u32[]{:S(2)}, u32[]{:S(2)}) collective-permute-start(bf16[96,256]{1,0:T(8,128)(2,1)S(1)} %get-tuple-element.16), channel_id=1, source_target_pairs={{0,8},{8,0},{1,9},{9,1},{2,10},{10,2},{3,11},{11,3},{4,12},{12,4},... | collective-permute-start | bytes 147464 | tf_op jit(solution)/shard_map/ppermute | solution.py:181
  20.0 0.9 collective-permute-done.1
  20.9 1.0 copy-done.3
  21.9 1.8 pad_maximum_fusion
  23.7 5.1 %all-to-all-done = bf16[32,24,256]{2,1,0:T(8,128)(2,1)S(1)} async-done(((bf16[32,24,256]{2,1,0:T(8,128)(2,1)}), bf16[32,24,256]{2,1,0:T(8,128)(2,1)S(1)}, u32[]{:S(2)}, u32[]{:S(2)}) %all-to-all-start) | async-done | bytes 393248 | tf_op jit(solution)/shard_map/all_to_all | solution.py:185
  29.5 28.9 %all_to_all.30.partial_ref = bf16[8,192,256]{2,1,0:T(8,128)(2,1)S(1)} all-to-all(bf16[8,192,256]{2,1,0:T(8,128)(2,1)S(1)} %first_queries.1), channel_id=1, replica_groups=mesh['q'=32,'c'=2,'far'=4,'near'=2] {'far','near'}, dimensions={0} | all-to-all | bytes 1572864 | tf_op jit(solution)/shard_map/all_to_all | solution.py:204
  58.8 4.4 %all_gather.26 = bf16[384,256]{1,0:T(8,128)(2,1)S(1)} all-gather(bf16[192,256]{1,0:T(8,128)(2,1)S(1)} %get-tuple-element.13), channel_id=1, replica_groups=mesh['q'=32,'c'=2,'far'=4,'near'=2] {'near'}, dimensions={0}, use_global_device_ids=true | all-gather | bytes 294912 | tf_op jit(solution)/shard_map/all_gather | solution.py:198
  63.2 15.5 %all_gather.27 = bf16[1536,256]{1,0:T(8,128)(2,1)S(1)} all-gather(bf16[384,256]{1,0:T(8,128)(2,1)S(1)} %all_gather.26), channel_id=1, replica_groups=mesh['q'=32,'c'=2,'far'=4,'near'=2] {'far'}, dimensions={0}, use_global_device_ids=true | all-gather | bytes 983040 | tf_op jit(solution)/shard_map/all_gather | solution.py:199
  78.7 0.8 convolution_convert_fusion.1
  79.5 21.1 %all_to_all.31.received_ref = bf16[32,24,256]{2,1,0:T(8,128)(2,1)S(1)} all-to-all(bf16[32,24,256]{2,1,0:T(8,128)(2,1)S(1)} %bitcast.23), channel_id=1, replica_groups=mesh['q'=32,'c'=2,'far'=4,'near'=2] {'q'}, dimensions={0} | all-to-all | bytes 786432 | tf_op jit(solution)/shard_map/all_to_all | solution.py:185
  100.7 15.3 %all_to_all.32 = bf16[32,24,256]{2,1,0:T(8,128)(2,1)S(1)} all-to-all(bf16[32,24,256]{2,1,0:T(8,128)(2,1)S(1)} %pack.1), channel_id=1, replica_groups=mesh['q'=32,'c'=2,'far'=4,'near'=2] {'q'}, dimensions={0} | all-to-all | bytes 786432 | tf_op jit(solution)/shard_map/all_to_all | solution.py:185
  116.0 0.8 second_queries.1
  116.8 18.8 %all_to_all.33.received_ref.partial_ref = bf16[8,200,256]{2,1,0:T(8,128)(2,1)S(1)} all-to-all(bf16[8,200,256]{2,1,0:T(8,128)(2,1)S(1)} %second_queries.1), channel_id=1, replica_groups=mesh['q'=32,'c'=2,'far'=4,'near'=2] {'far','near'}, dimensions={0} | all-to-all | bytes 1638400 | tf_op jit(solution)/shard_map/all_to_all | solution.py:211
  135.7 11.7 %all_gather.28.refs_0_ = f32[16,128]{1,0:T(8,128)S(1)} all-gather(f32[8,128]{1,0:T(8,128)S(1)} %total.1), channel_id=1, replica_groups=mesh['q'=32,'c'=2,'far'=4,'near'=2] {'c'}, dimensions={0}, use_global_device_ids=true | all-gather | bytes 12288 | tf_op jit(solution)/shard_map/all_gather | solution.py:213
  147.8 4.8 %all_gather.29 = bf16[384,256]{1,0:T(8,128)(2,1)S(1)} all-gather(bf16[192,256]{1,0:T(8,128)(2,1)S(1)} %second_heads.1), channel_id=1, replica_groups=mesh['q'=32,'c'=2,'far'=4,'near'=2] {'near'}, dimensions={0}, use_global_device_ids=true | all-gather | bytes 294912 | tf_op jit(solution)/shard_map/all_gather | solution.py:198
  152.5 14.9 %all_gather.30 = bf16[1536,256]{1,0:T(8,128)(2,1)S(1)} all-gather(bf16[384,256]{1,0:T(8,128)(2,1)S(1)} %all_gather.29), channel_id=1, replica_groups=mesh['q'=32,'c'=2,'far'=4,'near'=2] {'far'}, dimensions={0}, use_global_device_ids=true | all-gather | bytes 983040 | tf_op jit(solution)/shard_map/all_gather | solution.py:199
  167.5 0.8 convolution_convert_fusion
  168.3 15.2 %all_to_all.34.received_ref = bf16[32,24,256]{2,1,0:T(8,128)(2,1)S(1)} all-to-all(bf16[32,24,256]{2,1,0:T(8,128)(2,1)S(1)} %bitcast.22), channel_id=1, replica_groups=mesh['q'=32,'c'=2,'far'=4,'near'=2] {'q'}, dimensions={0} | all-to-all | bytes 786432 | tf_op jit(solution)/shard_map/all_to_all | solution.py:185
  183.6 8.3 %all_gather.31.second_ref = f32[48,256]{1,0:T(8,128)S(1)} all-gather(f32[24,256]{1,0:T(8,128)S(1)} %fold.1), channel_id=1, replica_groups=mesh['q'=32,'c'=2,'far'=4,'near'=2] {'c'}, dimensions={0}, use_global_device_ids=true | all-gather | bytes 73728 | tf_op jit(solution)/shard_map/all_gather | solution.py:223
  (16 shorter events, 2.5 us)
Async XLA Ops:
  10.0 10.8 %collective-permute-start = (bf16[768,768]{1,0:T(8,128)(2,1)}, bf16[768,768]{1,0:T(8,128)(2,1)S(1)}, u32[]{:S(2)}, u32[]{:S(2)}) collective-permute-start(bf16[768,768]{1,0:T(8,128)(2,1)} %param.5), channel_id=1, source_target_pairs={{0,8},{8,0},{1,9},{9,1},{2,10},{10,2},{3,11},{11,3},{4,12},{12,4},... | collective-permute-start | bytes 3538952 | tf_op jit(solution)/shard_map/ppermute | solution.py:174
  12.3 16.5 %all-to-all-start = ((bf16[32,24,256]{2,1,0:T(8,128)(2,1)}), bf16[32,24,256]{2,1,0:T(8,128)(2,1)S(1)}, u32[]{:S(2)}, u32[]{:S(2)}) async-start(bf16[32,24,256]{2,1,0:T(8,128)(2,1)} %spread.1), calls=%async_computation | async-start | bytes 786432 | tf_op jit(solution)/shard_map/all_to_all | solution.py:185
  17.7 3.1 %collective-permute-start.1 = (bf16[96,256]{1,0:T(8,128)(2,1)S(1)}, bf16[96,256]{1,0:T(8,128)(2,1)S(1)}, u32[]{:S(2)}, u32[]{:S(2)}) collective-permute-start(bf16[96,256]{1,0:T(8,128)(2,1)S(1)} %get-tuple-element.16), channel_id=1, source_target_pairs={{0,8},{8,0},{1,9},{9,1},{2,10},{10,2},{3,11},{11,3},{4,12},{12,4},... | collective-permute-start | bytes 147464 | tf_op jit(solution)/shard_map/ppermute | solution.py:181
  20.9 1.0 copy-start.3
  167.4 24.5 %copy-start = (f32[12,512]{1,0:T(8,128)S(1)}, f32[12,512]{1,0:T(8,128)}, u32[]{:S(2)}) copy-start(f32[12,512]{1,0:T(8,128)} %weights_ref.1) | copy-start | bytes 73732
  167.5 24.5 %copy-start.1 = (f32[12,512]{1,0:T(8,128)S(1)}, f32[12,512]{1,0:T(8,128)}, u32[]{:S(2)}) copy-start(f32[12,512]{1,0:T(8,128)} %one_ref.1) | copy-start | bytes 73732
  167.5 24.5 %copy-start.2 = (f32[12,512]{1,0:T(8,128)S(1)}, f32[12,512]{1,0:T(8,128)}, u32[]{:S(2)}) copy-start(f32[12,512]{1,0:T(8,128)} %two_ref.1) | copy-start | bytes 73732

commit v6 on v5

--- a/solution.py
+++ b/solution.py
@@ -12,7 +12,7 @@
 HEAD_DIM = 128
 TAIL = 8
 CORES = 2
-MP = ("far", "near")
+MP = ("near", "far")
 VMEM_BYTES = 16 * 1024 * 1024
 
 radius = 8.0
@@ -195,8 +195,8 @@
         )
 
     def gradient_of(grads):
+        grads = lax.all_gather(grads, "far", axis=0, tiled=True)
         grads = lax.all_gather(grads, "near", axis=0, tiled=True)
-        grads = lax.all_gather(grads, "far", axis=0, tiled=True)
         summed = lax.dot_general(tokens, grads, (((0,), (0,)), ((), ())), preferred_element_type=F32)
         return exchange(summed.astype(BF16).reshape(groups, CORES * rows, width))
 
@@ -228,8 +228,9 @@
 def solution(mesh):
     groups = mesh.shape["dp"] // CORES
     far = mesh.shape["mp"] // 2
-    fine = Mesh(mesh.devices.reshape(groups, CORES, far, 2), ("q", "c") + MP)
+    place = ("far", "near")
+    fine = Mesh(mesh.devices.reshape(groups, CORES, far, 2), ("q", "c") + place)
     dp = ("q", "c")
-    shard = P(MP + dp, None)
-    in_specs = (P(dp, MP), P(dp, None), shard, shard, shard)
+    shard = P(place + dp, None)
+    in_specs = (P(dp, place), P(dp, None), shard, shard, shard)
     return jax.shard_map(local, mesh=fine, in_specs=in_specs, out_specs=(shard,) * 3, check_vma=False)

time: 193 us -> 192 us (level)
    all_gather x2, blocking collectives: 9.13 us -> 16.7 us  [gradient_of(): grads = lax.all_gather(grads, 'near', axis=0, tiled=True)]
    all_gather x2, blocking collectives: 30.4 us -> 25.2 us  [gradient_of(): grads = lax.all_gather(grads, 'far', axis=0, tiled=True)]
  transfers between devices with their start and end apart: 3 -> 3, of which waited for: 2 -> 2; matrix products, arithmetic and copies ran while one was open for 1% -> 2% of each run, Pallas kernels for 0% -> 0%
where the time goes in v6:
time: 192 us; the launch traced here: 191 us
  blocking collectives  166 us (86%)
  starting transfers between devices  8.83 us (5%)
  waiting for transfers between devices  5.95 us (3%)
  Pallas kernels  4.05 us (2%)
  local copies, waits for them, and re-layouts  2.12 us (1%)
    all_to_all x3, blocking collectives, exchange(): return lax.all_to_all(blocks, 'q', 0, 0)  50.3 us
    all_to_all x2, blocking collectives, local(): received = lax.all_to_all(sent, MP, 0, 0)  46.7 us
    all_gather x2, blocking collectives, gradient_of(): grads = lax.all_gather(grads, 'far', axis=0, tiled=True)  25.2 us
    all_gather x2, blocking collectives, gradient_of(): grads = lax.all_gather(grads, 'near', axis=0, tiled=True)  16.7 us
    all_gather x1, blocking collectives, local(): squares = lax.all_gather(squares, 'c', axis=0, tiled=True)  10.6 us
    all_gather x1, blocking collectives, local(): lax.all_gather(weights, 'c', axis=0)  8.6 us
    all_gather x1, blocking collectives, local(): second = lax.all_gather(second, 'c', axis=0, tiled=True)  7.92 us
    all_to_all x1, waiting for transfers between devices, exchange(): return lax.all_to_all(blocks, 'q', 0, 0)  5.08 us
  transfers between devices with their start and end apart: 3, of which 2 were waited for; matrix products, arithmetic and copies ran while one was open for 2% of the time, Pallas kernels for 0%

profile of v6, /device:TPU:1, one launch (start us, length us, event | category | flops | bytes accessed | tf_op | source)
XLA Modules:
  0.0 191.2 jit_solution(14956401622150456451)
XLA Ops:
  0.6 8.6 %all-gather.1.weights_ref = f32[2,12,512]{2,1,0:T(8,128)S(1)} all-gather(f32[1,12,512]{2,1,0:T(8,128)} %bitcast.19), channel_id=2, replica_groups=mesh['q'=32,'c'=2,'far'=4,'near'=2] {'c'}, dimensions={0}, use_global_device_ids=true | all-gather | bytes 73728 | tf_op jit(solution)/shard_map/all_gather | solution.py:171
  9.2 0.8 spread.1
  10.0 2.2 %collective-permute-start = (bf16[768,768]{1,0:T(8,128)(2,1)}, bf16[768,768]{1,0:T(8,128)(2,1)S(1)}, u32[]{:S(2)}, u32[]{:S(2)}) collective-permute-start(bf16[768,768]{1,0:T(8,128)(2,1)} %param.5), channel_id=1, source_target_pairs={{0,8},{8,0},{1,9},{9,1},{2,10},{10,2},{3,11},{11,3},{4,12},{12,4},... | collective-permute-start | bytes 3538952 | tf_op jit(solution)/shard_map/ppermute | solution.py:174
  12.3 4.3 %all-to-all-start = ((bf16[32,24,256]{2,1,0:T(8,128)(2,1)}), bf16[32,24,256]{2,1,0:T(8,128)(2,1)S(1)}, u32[]{:S(2)}, u32[]{:S(2)}) async-start(bf16[32,24,256]{2,1,0:T(8,128)(2,1)} %spread.1), calls=%async_computation | async-start | bytes 786432 | tf_op jit(solution)/shard_map/all_to_all | solution.py:185
  16.6 1.1 fusion
  17.7 2.3 %collective-permute-start.1 = (bf16[96,256]{1,0:T(8,128)(2,1)S(1)}, bf16[96,256]{1,0:T(8,128)(2,1)S(1)}, u32[]{:S(2)}, u32[]{:S(2)}) collective-permute-start(bf16[96,256]{1,0:T(8,128)(2,1)S(1)} %get-tuple-element.16), channel_id=1, source_target_pairs={{0,8},{8,0},{1,9},{9,1},{2,10},{10,2},{3,11},{11,3},{4,12},{12,4},... | collective-permute-start | bytes 147464 | tf_op jit(solution)/shard_map/ppermute | solution.py:181
  20.0 0.9 collective-permute-done.1
  20.9 1.0 copy-done.3
  21.9 1.8 pad_maximum_fusion
  23.7 5.1 %all-to-all-done = bf16[32,24,256]{2,1,0:T(8,128)(2,1)S(1)} async-done(((bf16[32,24,256]{2,1,0:T(8,128)(2,1)}), bf16[32,24,256]{2,1,0:T(8,128)(2,1)S(1)}, u32[]{:S(2)}, u32[]{:S(2)}) %all-to-all-start) | async-done | bytes 393248 | tf_op jit(solution)/shard_map/all_to_all | solution.py:185
  29.5 26.7 %all_to_all.30.partial_ref = bf16[8,192,256]{2,1,0:T(8,128)(2,1)S(1)} all-to-all(bf16[8,192,256]{2,1,0:T(8,128)(2,1)S(1)} %first_queries.1), channel_id=1, replica_groups=mesh['q'=32,'c'=2,'far'=4,'near'=2] {'near','far'}, dimensions={0} | all-to-all | bytes 1572864 | tf_op jit(solution)/shard_map/all_to_all | solution.py:204
  56.6 12.9 %all_gather.26 = bf16[768,256]{1,0:T(8,128)(2,1)S(1)} all-gather(bf16[192,256]{1,0:T(8,128)(2,1)S(1)} %get-tuple-element.13), channel_id=1, replica_groups=mesh['q'=32,'c'=2,'far'=4,'near'=2] {'far'}, dimensions={0}, use_global_device_ids=true | all-gather | bytes 491520 | tf_op jit(solution)/shard_map/all_gather | solution.py:198
  69.5 8.5 %all_gather.27 = bf16[1536,256]{1,0:T(8,128)(2,1)S(1)} all-gather(bf16[768,256]{1,0:T(8,128)(2,1)S(1)} %all_gather.26), channel_id=1, replica_groups=mesh['q'=32,'c'=2,'far'=4,'near'=2] {'near'}, dimensions={0}, use_global_device_ids=true | all-gather | bytes 1179648 | tf_op jit(solution)/shard_map/all_gather | solution.py:199
  78.0 0.8 convolution_convert_fusion.1
  78.9 19.3 %all_to_all.31.received_ref = bf16[32,24,256]{2,1,0:T(8,128)(2,1)S(1)} all-to-all(bf16[32,24,256]{2,1,0:T(8,128)(2,1)S(1)} %bitcast.23), channel_id=1, replica_groups=mesh['q'=32,'c'=2,'far'=4,'near'=2] {'q'}, dimensions={0} | all-to-all | bytes 786432 | tf_op jit(solution)/shard_map/all_to_all | solution.py:185
  98.2 15.5 %all_to_all.32 = bf16[32,24,256]{2,1,0:T(8,128)(2,1)S(1)} all-to-all(bf16[32,24,256]{2,1,0:T(8,128)(2,1)S(1)} %pack.1), channel_id=1, replica_groups=mesh['q'=32,'c'=2,'far'=4,'near'=2] {'q'}, dimensions={0} | all-to-all | bytes 786432 | tf_op jit(solution)/shard_map/all_to_all | solution.py:185
  113.8 0.8 second_queries.1
  114.6 19.9 %all_to_all.33.received_ref.partial_ref = bf16[8,200,256]{2,1,0:T(8,128)(2,1)S(1)} all-to-all(bf16[8,200,256]{2,1,0:T(8,128)(2,1)S(1)} %second_queries.1), channel_id=1, replica_groups=mesh['q'=32,'c'=2,'far'=4,'near'=2] {'near','far'}, dimensions={0} | all-to-all | bytes 1638400 | tf_op jit(solution)/shard_map/all_to_all | solution.py:211
  134.7 10.6 %all_gather.28.refs_0_ = f32[16,128]{1,0:T(8,128)S(1)} all-gather(f32[8,128]{1,0:T(8,128)S(1)} %total.1), channel_id=1, replica_groups=mesh['q'=32,'c'=2,'far'=4,'near'=2] {'c'}, dimensions={0}, use_global_device_ids=true | all-gather | bytes 12288 | tf_op jit(solution)/shard_map/all_gather | solution.py:213
  145.7 12.3 %all_gather.29 = bf16[768,256]{1,0:T(8,128)(2,1)S(1)} all-gather(bf16[192,256]{1,0:T(8,128)(2,1)S(1)} %second_heads.1), channel_id=1, replica_groups=mesh['q'=32,'c'=2,'far'=4,'near'=2] {'far'}, dimensions={0}, use_global_device_ids=true | all-gather | bytes 491520 | tf_op jit(solution)/shard_map/all_gather | solution.py:198
  158.0 8.3 %all_gather.30 = bf16[1536,256]{1,0:T(8,128)(2,1)S(1)} all-gather(bf16[768,256]{1,0:T(8,128)(2,1)S(1)} %all_gather.29), channel_id=1, replica_groups=mesh['q'=32,'c'=2,'far'=4,'near'=2] {'near'}, dimensions={0}, use_global_device_ids=true | all-gather | bytes 1179648 | tf_op jit(solution)/shard_map/all_gather | solution.py:199
  166.2 0.8 convolution_convert_fusion
  167.1 15.5 %all_to_all.34.received_ref = bf16[32,24,256]{2,1,0:T(8,128)(2,1)S(1)} all-to-all(bf16[32,24,256]{2,1,0:T(8,128)(2,1)S(1)} %bitcast.22), channel_id=1, replica_groups=mesh['q'=32,'c'=2,'far'=4,'near'=2] {'q'}, dimensions={0} | all-to-all | bytes 786432 | tf_op jit(solution)/shard_map/all_to_all | solution.py:185
  182.6 7.9 %all_gather.31.second_ref = f32[48,256]{1,0:T(8,128)S(1)} all-gather(f32[24,256]{1,0:T(8,128)S(1)} %fold.1), channel_id=1, replica_groups=mesh['q'=32,'c'=2,'far'=4,'near'=2] {'c'}, dimensions={0}, use_global_device_ids=true | all-gather | bytes 73728 | tf_op jit(solution)/shard_map/all_gather | solution.py:223
  (16 shorter events, 2.5 us)
Async XLA Ops:
  10.0 10.8 %collective-permute-start = (bf16[768,768]{1,0:T(8,128)(2,1)}, bf16[768,768]{1,0:T(8,128)(2,1)S(1)}, u32[]{:S(2)}, u32[]{:S(2)}) collective-permute-start(bf16[768,768]{1,0:T(8,128)(2,1)} %param.5), channel_id=1, source_target_pairs={{0,8},{8,0},{1,9},{9,1},{2,10},{10,2},{3,11},{11,3},{4,12},{12,4},... | collective-permute-start | bytes 3538952 | tf_op jit(solution)/shard_map/ppermute | solution.py:174
  12.3 16.5 %all-to-all-start = ((bf16[32,24,256]{2,1,0:T(8,128)(2,1)}), bf16[32,24,256]{2,1,0:T(8,128)(2,1)S(1)}, u32[]{:S(2)}, u32[]{:S(2)}) async-start(bf16[32,24,256]{2,1,0:T(8,128)(2,1)} %spread.1), calls=%async_computation | async-start | bytes 786432 | tf_op jit(solution)/shard_map/all_to_all | solution.py:185
  17.7 3.1 %collective-permute-start.1 = (bf16[96,256]{1,0:T(8,128)(2,1)S(1)}, bf16[96,256]{1,0:T(8,128)(2,1)S(1)}, u32[]{:S(2)}, u32[]{:S(2)}) collective-permute-start(bf16[96,256]{1,0:T(8,128)(2,1)S(1)} %get-tuple-element.16), channel_id=1, source_target_pairs={{0,8},{8,0},{1,9},{9,1},{2,10},{10,2},{3,11},{11,3},{4,12},{12,4},... | collective-permute-start | bytes 147464 | tf_op jit(solution)/shard_map/ppermute | solution.py:181
  20.9 1.0 copy-start.3
  166.2 24.3 %copy-start = (f32[12,512]{1,0:T(8,128)S(1)}, f32[12,512]{1,0:T(8,128)}, u32[]{:S(2)}) copy-start(f32[12,512]{1,0:T(8,128)} %weights_ref.1) | copy-start | bytes 73732
  166.2 24.3 %copy-start.1 = (f32[12,512]{1,0:T(8,128)S(1)}, f32[12,512]{1,0:T(8,128)}, u32[]{:S(2)}) copy-start(f32[12,512]{1,0:T(8,128)} %one_ref.1) | copy-start | bytes 73732
  166.2 24.3 %copy-start.2 = (f32[12,512]{1,0:T(8,128)S(1)}, f32[12,512]{1,0:T(8,128)}, u32[]{:S(2)}) copy-start(f32[12,512]{1,0:T(8,128)} %two_ref.1) | copy-start | bytes 73732
